TPU v7x, 32 devices: a whole 2x2x4 slice. The times are simulated.
32 devices in a mesh: tiles: 2 (over y), date: 4 (over z), space: 4 (over x, core).
Axes of the slice: x: 2, y: 2, z: 4, core: 2. Of those that a mesh axis runs over, the one named last changes fastest.
Arguments:
- reflect: float32 [8, 6, 8192], P('date', None, ('tiles', 'space')), parts along dimension 2, may hold values from -0.05 to 1.05
- clear_sky: int32 [8, 8192], P('date', ('tiles', 'space')), parts along dimension 1, may hold values 0 or 1
- live_dates: int32 [4], replicated, may hold values from 1 to 2, as said below
- day_of_year: int32 [8], replicated, may hold values from 1 to 365
- ref_quantile: float32 [6, 256], replicated, may hold values from 0 to 1, as said below
Outputs:
- residual: float32 [8, 6, 8192], P('date', None, ('tiles', 'space')), parts along dimension 2
There are 2 independent parts, one for each index of `tiles`. A program takes and returns all parts, laid end to end along the dimension named above; an argument that names none is the same for every part. Nothing has to cross between parts.
Inputs may be any that keep to these rules, and one draw needn't show every extreme that they name: `live_dates`: some group has all 2 slots live and some group has exactly 1. `ref_quantile`: strictly increasing along the bins.
All inputs are finite; a program needn't handle non-finite values. No bound on the sum of `clear_sky` on one device may be relied on, other than what follows from the above.
Results may differ from a plain program's by a relative error of at most 0.009.
Values sent between devices are 32-bit elements; how exact they have to be, the bound alone decides.
A program may use at most 64 MiB of HBM per device.

v0:
```python
import math

import jax
import jax.numpy as jnp
from jax import lax
from jax.sharding import PartitionSpec as P

ridge_weight = 1.0
year_days = 365.0


def tent_weights(position, bin_count):
    centers = jnp.arange(bin_count, dtype=jnp.float32)
    return jnp.maximum(0.0, 1.0 - jnp.abs(position[..., None] - centers)).astype(jnp.bfloat16)


def harmonic_basis(day_of_year, harmonics):
    angles = 2.0 * math.pi * day_of_year.astype(jnp.float32) / year_days
    orders = jnp.arange(1, harmonics + 1, dtype=jnp.float32)
    phases = angles[:, None] * orders[None, :]
    ones_col = jnp.ones((day_of_year.shape[0], 1), jnp.float32)
    return jnp.concatenate([ones_col, jnp.cos(phases), jnp.sin(phases)], axis=1)


def per_device(reflect, clear_sky, live_dates, day_of_year, ref_quantile):
    date_slots, band_count, pixels = reflect.shape
    bin_count = ref_quantile.shape[1]
    groups = lax.axis_size("date")
    device = lax.axis_index("date")
    date_count = date_slots * groups
    slot_index = jnp.arange(date_count, dtype=jnp.int32)
    counts_each = jnp.repeat(live_dates, date_slots)
    live_flag = (slot_index % date_slots < counts_each).astype(jnp.float32)
    own_flag = lax.dynamic_slice_in_dim(live_flag, device * date_slots, date_slots, 0)
    valid_mask = clear_sky * own_flag.astype(jnp.int32)[:, None]
    valid_half = valid_mask.astype(jnp.bfloat16)
    block_width = min(256, pixels)
    blocks = pixels // block_width

    def add_block(block_index, totals):
        values = lax.dynamic_slice_in_dim(reflect, block_index * block_width, block_width, 2)
        mask_part = lax.dynamic_slice_in_dim(valid_half, block_index * block_width, block_width, 1)
        weights = tent_weights(jnp.clip(bin_count * values - 0.5, 0.0, bin_count - 1.0), bin_count)
        return totals + jnp.einsum(
            "dbpk,dp->dbk", weights, mask_part, preferred_element_type=jnp.float32
        )

    histogram = lax.fori_loop(
        0, blocks, add_block, jnp.zeros((date_slots, band_count, bin_count), jnp.float32)
    )
    histogram = lax.psum(histogram, "space")
    grand_total = jnp.maximum(jnp.sum(histogram, axis=-1, keepdims=True), 1.0)
    cumulative = ((jnp.cumsum(histogram, axis=-1) - 0.5 * histogram) / grand_total).astype(
        jnp.bfloat16
    )
    quant_half = ref_quantile.astype(jnp.bfloat16)

    def match_block(block_index, matched):
        values = lax.dynamic_slice_in_dim(reflect, block_index * block_width, block_width, 2)
        weights = tent_weights(jnp.clip(bin_count * values - 0.5, 0.0, bin_count - 1.0), bin_count)
        level_pos = jnp.einsum(
            "dbpk,dbk->dbp", weights, cumulative, preferred_element_type=jnp.float32
        )
        level_pos = jnp.clip(bin_count * level_pos - 0.5, 0.0, bin_count - 1.0)
        second = tent_weights(level_pos, bin_count)
        result = jnp.einsum("dbpk,bk->dbp", second, quant_half, preferred_element_type=jnp.float32)
        return lax.dynamic_update_slice_in_dim(matched, result, block_index * block_width, 2)

    matched = lax.fori_loop(
        0, blocks, match_block, jnp.zeros((date_slots, band_count, pixels), jnp.float32)
    )
    design = harmonic_basis(day_of_year, ref_quantile.shape[0] * 0 + 7)
    coef_count = design.shape[1]
    weighted_design = design * live_flag[:, None]
    normal = jnp.dot(
        weighted_design.T, design, precision=lax.Precision.HIGHEST
    ) + ridge_weight * jnp.eye(coef_count, dtype=jnp.float32)
    factor = jnp.linalg.cholesky(normal)
    projector = jax.scipy.linalg.cho_solve((factor, True), weighted_design.T)
    series, mask_series = (
        lax.all_to_all(matched, "date", split_axis=2, concat_axis=0, tiled=True),
        lax.all_to_all(valid_mask[:, None, :], "date", split_axis=2, concat_axis=0, tiled=True),
    )
    mask_float = mask_series.astype(jnp.float32)
    valid_count = jnp.sum(mask_float, axis=0)
    fill_mean = jnp.sum(mask_float * series, axis=0) / jnp.maximum(valid_count, 1.0)
    filled = mask_float * series + (1.0 - mask_float) * fill_mean[None]
    stacked = filled.reshape(date_count, -1)
    coefficients = jnp.dot(projector, stacked, precision=lax.Precision.HIGHEST)
    fitted = jnp.dot(design, coefficients, precision=lax.Precision.HIGHEST).reshape(series.shape)
    leftover = mask_float * (series - fitted)
    residual = lax.all_to_all(leftover, "date", split_axis=0, concat_axis=2, tiled=True)
    return residual


def solution(mesh):
    return jax.shard_map(
        per_device,
        mesh=mesh,
        in_specs=(
            P("date", None, ("tiles", "space")),
            P("date", ("tiles", "space")),
            P(),
            P(),
            P(),
        ),
        out_specs=P("date", None, ("tiles", "space")),
        check_vma=False,
    )
```

profile of v0, /device:TPU:0, one launch (start us, length us, event | category | flops | bytes accessed | tf_op | source)
XLA Modules:
  0.0 67.1 jit_solution(741411858038961387)
XLA Ops:
  0.0 0.7 %broadcast_in_dim.36 = s32[4,2]{1,0:T(4,128)S(1)} broadcast(s32[4]{0:T(128)} %param.11), dimensions={0} | broadcast | bytes 48 | tf_op jit(solution)/shard_map/broadcast_in_dim | solution.py:32
  0.7 0.1 reshape.106
  0.8 0.9 %copy.68 = s32[2,1024]{0,1:T(8,128)S(1)} copy(s32[2,1024]{1,0:T(2,128)} %param.10) | data formatting | bytes 16384 | tf_op args[1]
  1.7 0.1 dynamic-slice_convert_fusion
  1.8 0.1 fusion.31
  1.9 0.0 copy-start.2
  1.9 0.0 copy-start.1
  1.9 0.5 broadcast.286
  2.4 1.9 %reduce.14 = s32[1024,2]{1,0:T(8,128)S(1)} reduce(s32[1024,1,2]{2,1,0:T(1,128)S(1)} %bitcast.83, s32[]{:T(128)} %broadcast.286), dimensions={1}, to_apply=%bitcast.60.reduce_sub_computation | reduce | bytes 16388
  4.3 0.9 %reshape.119 = s32[4,1,512]{2,1,0:T(1,128)} reshape(s32[1024,2]{1,0:T(8,128)S(1)} %reduce.14) | data formatting | bytes 16384
  5.2 6.3 %all-to-all-start = ((s32[4,1,512]{2,1,0:T(1,128)}), s32[4,1,512]{2,1,0:T(1,128)S(1)}, u32[]{:S(2)}, u32[]{:S(2)}) async-start(s32[4,1,512]{2,1,0:T(1,128)} %reshape.119), calls=%async_computation | async-start | bytes 16384 | tf_op jit(solution)/shard_map/all_to_all | solution.py:82
  11.5 0.0 copy-done.2
  11.6 0.0 copy-done.1
  11.6 0.1 multiply_cosine_fusion
  11.7 0.1 pad_maximum_fusion
  11.8 0.3 fusion.27
  12.1 0.1 copy.80
  12.2 1.4 %cholesky.17 = f32[15,15]{1,0:T(8,128)S(1)} custom-call(f32[15,15]{1,0:T(8,128)S(1)} %fusion.25), custom_call_target="Cholesky" | custom-call | tf_op jit(solution)/shard_map/jit(cholesky)/cholesky | solution.py:78
  13.6 0.7 %compare_reduce_fusion = pred[]{:T(512)} fusion(f32[15]{0:T(128)S(1)} %select_reduce_fusion), kind=kLoop, calls=%fused_computation.57 | loop fusion | flops 29 | bytes 61 | tf_op jit(solution)/shard_map/jit(cholesky)/cholesky | solution.py:78
  14.3 0.6 fusion.19
  14.9 1.2 %custom-call.10 = f32[1,15,15]{1,2,0:T(8,128)S(1)} custom-call(f32[1,15,15]{2,1,0:T(8,128)S(1)} %fusion.19), custom_call_target="InvertDiagBlocksLowerTriangular" | custom-call | tf_op jit(solution)/shard_map/jit(_cho_solve)/triangular_solve | solution.py:79
  16.1 0.2 fusion.22
  16.3 0.2 copy.70
  16.4 2.9 %while.33 = (s32[]{:T(128)}, f32[2,6,256]{2,1,0:T(8,128)S(1)}, f32[2,6,1024]{2,0,1:T(2,128)S(1)}, bf16[2,1024]{1,0:T(2,128)(2,1)S(1)}, s32[]{:T(128)}, /*index=5*/s32[]{:T(128)}, s32[]{:T(128)}, s32[]{:T(128)}) while((s32[]{:T(128)}, f32[2,6,256]{2,1,0:T(8,128)S(1)}, f32[2,6,1024]{2,0,1:T(2,128)S(1)}, ...), condition=%wide.region_1.2_spmd.clone, body=%wide.region_0.1_spmd.clone.sunk | while | flops 5520391 | bytes 113821 | solution.py:48
  16.5 0.7 fusion.53
  17.2 0.7 fusion.53
  17.9 0.7 fusion.53
  18.7 0.7 fusion.53
  19.4 10.6 %psum.7 = f32[2,6,256]{2,0,1:T(2,128)S(1)} all-reduce(f32[2,6,256]{2,0,1:T(2,128)S(1)} %copy.71), channel_id=1, replica_groups=mesh['tiles'=2,'date'=4,'space'=4] {'space'}, use_global_device_ids=true, to_apply=%region_2.3 | all-reduce | flops 3072 | bytes 24576 | tf_op jit(solution)/shard_map/psum | solution.py:51
  30.0 0.1 reduce_sum.34
  30.1 3.6 %reduce-window.6 = f32[2,6,2,128]{3,2,1,0:T(2,128)S(1)} reduce-window(f32[2,6,2,128]{3,2,1,0:T(2,128)S(1)} %copy.72, f32[]{:T(128)} %constant.276.clone.1), window={size=1x1x1x128 pad=0_0x0_0x0_0x127_0}, to_apply=%region_3.4 | reduce-window | flops 390144 | bytes 24580 | tf_op jit(solution)/shard_map/reduce-window
  33.7 0.1 slice.26
  33.8 0.1 copy.73
  33.9 0.1 copy.74
  34.0 0.1 broadcast_add_fusion
  34.2 0.1 fusion.18
  34.3 5.5 %while.32 = (s32[]{:T(128)}, f32[2,6,1024]{2,1,0:T(8,128)S(1)}, f32[2,6,1024]{2,0,1:T(2,128)S(1)}, bf16[2,6,256]{2,1,0:T(8,128)(2,1)S(1)}, bf16[6,256]{1,0:T(8,1...) while((s32[]{:T(128)}, f32[2,6,1024]{2,1,0:T(8,128)S(1)}, f32[2,6,1024]{2,0,1:T(2,128)S(1)}, ...), condition=%wide.region_7.8_spmd, body=%wide.region_6.7_spmd.sunk | while | flops 11028486 | bytes 185491 | solution.py:69
  34.3 0.6 fusion.49
  35.0 0.6 fusion.51
  35.7 0.6 fusion.49
  36.4 0.6 fusion.51
  37.0 0.6 fusion.49
  37.7 0.6 fusion.51
  38.4 0.6 fusion.49
  39.1 0.6 fusion.51
  39.7 0.1 fusion.20
  39.9 0.6 copy.77
  40.4 2.1 %reshape.117 = f32[4,1,3072]{2,1,0:T(1,128)} reshape(f32[1024,2,6]{2,1,0:T(2,128)S(1)} %bitcast.81) | data formatting | bytes 98304
  42.6 0.0 all-to-all-done
  42.6 4.8 %all-to-all-start.1 = ((f32[4,1,3072]{2,1,0:T(1,128)}), f32[4,1,3072]{2,1,0:T(1,128)S(1)}, u32[]{:S(2)}, u32[]{:S(2)}) async-start(f32[4,1,3072]{2,1,0:T(1,128)} %reshape.117), calls=%async_computation.1 | async-start | bytes 98304 | tf_op jit(solution)/shard_map/all_to_all | solution.py:81
  47.4 0.6 reduce.15
  48.0 0.9 %reshape.120 = s32[1024,1,2]{2,1,0:T(1,128)S(1)} reshape(s32[4,512]{1,0:T(4,128)S(1)} %reduce.15) | data formatting | bytes 16384
  48.9 2.2 %convert_reduce_fusion = f32[1024]{0:T(1024)S(1)} fusion(s32[1024,1,2]{2,1,0:T(1,128)S(1)} %reshape.120), kind=kLoop, calls=%fused_computation.64 | loop fusion | flops 3072 | bytes 12288 | tf_op jit(solution)/shard_map/reduce_sum | solution.py:85
  51.0 0.4 bitcast_convert_fusion
  51.4 0.2 copy.69
  51.7 1.4 %all-to-all-done.1 = f32[4,1,3072]{2,1,0:T(1,128)S(1)} async-done(((f32[4,1,3072]{2,1,0:T(1,128)}), f32[4,1,3072]{2,1,0:T(1,128)S(1)}, u32[]{:S(2)}, u32[]{:S(2)}) %all-to-all-start.1) | async-done | bytes 49184 | tf_op jit(solution)/shard_map/all_to_all | solution.py:81
  53.1 0.5 broadcast.285
  53.6 0.8 %reduce.13 = f32[4,3072]{1,0:T(4,128)S(1)} reduce(f32[4,1,3072]{2,1,0:T(1,128)S(1)} %all-to-all-done.1, f32[]{:T(128)} %broadcast.285), dimensions={1}, to_apply=%all_to_all.36.reduce_sub_computation | reduce | bytes 98308 | tf_op jit(solution)/shard_map/all_to_all | solution.py:81
  54.4 1.6 %reshape.118 = f32[1024,2,6]{2,1,0:T(2,128)S(1)} reshape(f32[4,3072]{1,0:T(4,128)S(1)} %reduce.13) | data formatting | bytes 98304
  55.9 0.5 copy.92
  56.6 0.3 fusion.13
  56.9 0.2 fusion.32
  57.2 9.2 %all_to_all.48 = f32[8,6,256]{2,1,0:T(8,128)S(1)} all-to-all(f32[8,6,256]{2,1,0:T(8,128)S(1)} %copy.83), channel_id=1, replica_groups=mesh['tiles'=2,'date'=4,'space'=4] {'date'}, dimensions={0} | all-to-all | bytes 98304 | tf_op jit(solution)/shard_map/all_to_all | solution.py:92
  66.4 0.7 all_to_all.44
  (74 shorter events, 0.8 us)
Async XLA Ops:
  1.9 9.6 %copy-start.2 = (s32[8]{0:T(128)S(1)}, s32[8]{0:T(128)}, u32[]{:S(2)}) copy-start(s32[8]{0:T(128)} %param.12) | copy-start | bytes 100
  1.9 9.7 %copy-start.1 = (f32[6,256]{1,0:T(8,128)S(1)}, f32[6,256]{1,0:T(8,128)}, u32[]{:S(2)}) copy-start(f32[6,256]{1,0:T(8,128)} %param.13) | copy-start | bytes 18436
  2.4 14.0 %copy-start = (f32[2,6,1024]{2,0,1:T(2,128)S(1)}, f32[2,6,1024]{2,0,1:T(2,128)}, u32[]{:S(2)}) copy-start(f32[2,6,1024]{2,0,1:T(2,128)} %param.9) | copy-start | bytes 147460
  5.2 37.4 %all-to-all-start = ((s32[4,1,512]{2,1,0:T(1,128)}), s32[4,1,512]{2,1,0:T(1,128)S(1)}, u32[]{:S(2)}, u32[]{:S(2)}) async-start(s32[4,1,512]{2,1,0:T(1,128)} %reshape.119), calls=%async_computation | async-start | bytes 16384 | tf_op jit(solution)/shard_map/all_to_all | solution.py:82
  42.6 10.5 %all-to-all-start.1 = ((f32[4,1,3072]{2,1,0:T(1,128)}), f32[4,1,3072]{2,1,0:T(1,128)S(1)}, u32[]{:S(2)}, u32[]{:S(2)}) async-start(f32[4,1,3072]{2,1,0:T(1,128)} %reshape.117), calls=%async_computation.1 | async-start | bytes 98304 | tf_op jit(solution)/shard_map/all_to_all | solution.py:81
where the time goes:
time: 67.5 us; the launch traced here: 67.1 us
  blocking collectives  19.8 us (29%)
  other arithmetic  14.2 us (21%)
  local copies, waits for them, and re-layouts  11.1 us (16%)
  starting transfers between devices  11.1 us (16%)
  matrix products  8.85 us (13%)
  waiting for transfers between devices  1.44 us (2%)
    psum x1, blocking collectives, per_device(): histogram = lax.psum(histogram, 'space')  10.6 us
    all_to_all x1, blocking collectives, per_device(): lax.all_to_all(leftover, 'date', split_axis=0, concat_axis=2, tiled=True)  9.21 us
    unnamed x14, local copies, waits for them, and re-layouts  7.1 us
    all_to_all x1, starting transfers between devices, per_device(): lax.all_to_all(valid_mask[:, None, :], 'date', split_axis=2, concat_axis=...  6.32 us
    all_to_all x1, starting transfers between devices, per_device(): lax.all_to_all(matched, 'date', split_axis=2, concat_axis=0, tiled=True)  4.8 us
    another operation x3, other arithmetic  3.75 us
    dot_general x4, matrix products, add_block(): jnp.einsum('dbpk,dp->dbk', weights, mask_part, preferred_element_type=jnp...  2.66 us
    dot_general x4, matrix products, match_block(): jnp.einsum('dbpk,dbk->dbp', weights, cumulative, preferred_element_type=j...  2.57 us
  transfers between devices with their start and end apart: 2, of which 1 were waited for; matrix products, arithmetic and copies ran while one was open for 36% of the time, Pallas kernels for 0%

commit v1 on v0

v1 whole, which is shorter than its diff:
```python
import functools
import math

import jax
import jax.numpy as jnp
from jax import lax
from jax.experimental import pallas as pl
from jax.experimental.pallas import tpu as pltpu
from jax.sharding import PartitionSpec as P

MESH = pl.DeviceIdType.MESH
HARMONICS = 7
RIDGE = 1.0
YEAR = 365
LOW = 16
LANES = 128
SUBLANES = 8


def iota(shape, dim):
    return lax.broadcasted_iota(jnp.int32, shape, dim)


def rounded(x):
    return x.astype(jnp.bfloat16).astype(jnp.float32)


def block_histogram(values, valid, bands, bins):
    high_count = bins // LOW
    pixels = values.shape[1]
    position = jnp.clip(bins * values - 0.5, 0.0, bins - 1.0)
    high = jnp.floor(position * (1.0 / LOW))
    local = position - LOW * high
    marked = jnp.where(valid, high, -1.0)
    high_iota = iota((high_count, pixels), 0).astype(jnp.float32)
    low_iota = iota((LOW, pixels), 0).astype(jnp.float32)
    hot, tents = [], []
    for b in range(bands):
        hot.append(jnp.where(high_iota == marked[b : b + 1], 1.0, 0.0).astype(jnp.bfloat16))
        tents.append(
            jnp.maximum(0.0, 1.0 - jnp.abs(local[b : b + 1] - low_iota)).astype(jnp.bfloat16)
        )
    spill = jnp.maximum(0.0, 1.0 - jnp.abs(local - LOW))
    tents.append(jnp.concatenate([spill, jnp.zeros_like(spill)], axis=0).astype(jnp.bfloat16))
    hot.append(jnp.zeros((LANES - bands * high_count, pixels), jnp.bfloat16))
    counts = lax.dot_general(
        jnp.concatenate(tents, axis=0),
        jnp.concatenate(hot, axis=0),
        (((1,), (1,)), ((), ())),
        preferred_element_type=jnp.float32,
    )
    band_lane = iota((LOW, LANES), 1) // high_count
    inner = jnp.zeros((LOW, LANES), jnp.float32)
    for b in range(bands):
        inner += jnp.where(band_lane == b, counts[b * LOW : (b + 1) * LOW], 0.0)
    outer = counts[bands * LOW : bands * LOW + SUBLANES]
    own = iota((SUBLANES, LANES), 0) == band_lane[:SUBLANES]
    return inner, jnp.sum(jnp.where(own, outer, 0.0), axis=0, keepdims=True)


def running_sums(inner, spill, bands, bins):
    high_count = bins // LOW
    dates = len(inner)
    used = bands * high_count
    column = [jnp.sum(inner[d], axis=0, keepdims=True) + spill[d] for d in range(dates)]
    rows = column + spill
    left = jnp.zeros((SUBLANES, LANES), jnp.float32)
    row_of = iota((SUBLANES, LANES), 0)
    for i, row in enumerate(rows):
        left = jnp.where(row_of == i, row, left)
    src, dst = iota((LANES, LANES), 0), iota((LANES, LANES), 1)
    same = (src // high_count == dst // high_count) & (dst < used)
    before = jnp.where((same & (src < dst)) | (dst == used + src // high_count), 1.0, 0.0)
    shift = jnp.where(same & (src + 1 == dst), 0.5, 0.0)
    before = jnp.where(src < used, before, 0.0)
    shift = jnp.where(src < used, shift, 0.0)
    moved = jnp.dot(
        left,
        jnp.concatenate([before, shift], axis=1),
        precision=lax.Precision.HIGHEST,
        preferred_element_type=jnp.float32,
    )
    out_row, in_row = iota((LOW, LOW), 0), iota((LOW, LOW), 1)
    lower = jnp.where(in_row < out_row, 1.0, jnp.where(in_row == out_row, 0.5, 0.0))
    within = jnp.dot(
        lower,
        jnp.concatenate(inner, axis=1),
        precision=lax.Precision.HIGHEST,
        preferred_element_type=jnp.float32,
    )
    first = iota((LOW, LANES), 0) == 0
    sums = []
    for d in range(dates):
        part = within[:, d * LANES : (d + 1) * LANES] + moved[d : d + 1, :LANES]
        back = moved[dates + d : dates + d + 1, LANES:]
        sums.append(part - jnp.where(first, back, 0.0))
    return sums


def flat_table(sums, bands, bins):
    high_count = bins // LOW
    used = bands * high_count
    lane = iota((SUBLANES, LANES), 1)
    total_lane = jnp.minimum(used + lane // high_count, LANES - 1)
    total = jnp.take_along_axis(sums[:SUBLANES], total_lane, axis=1)[:1]
    cumulative = (sums / jnp.maximum(total, 1.0)).astype(jnp.bfloat16).astype(jnp.float32)
    band_lane = iota((LOW, LANES), 1) // high_count
    wide = jnp.concatenate(
        [jnp.where(band_lane == b, cumulative, 0.0) for b in range(bands)], axis=0
    ).astype(jnp.bfloat16)
    src, dst = iota((LANES, bins), 0), iota((LANES, bins), 1)
    spread = jnp.where((src % high_count == dst // LOW) & (src < used), 1.0, 0.0).astype(
        jnp.bfloat16
    )
    placed = jnp.dot(wide, spread, preferred_element_type=jnp.float32)
    rows, cols = iota(placed.shape, 0), iota(placed.shape, 1)
    placed = jnp.where(rows % LOW == cols % LOW, placed, 0.0).astype(jnp.bfloat16)
    pick = jnp.where(
        iota((SUBLANES, bands * LOW), 1) // LOW == iota((SUBLANES, bands * LOW), 0), 1.0, 0.0
    ).astype(jnp.bfloat16)
    return jnp.dot(pick, placed, preferred_element_type=jnp.float32)


def gather_lanes(table, index):
    parts = table.shape[1] // LANES
    inner = index % LANES
    out = jnp.take_along_axis(table[:, :LANES], inner, axis=1)
    for part in range(1, parts):
        other = jnp.take_along_axis(table[:, part * LANES : (part + 1) * LANES], inner, axis=1)
        out = jnp.where(index >= part * LANES, other, out)
    return out


def interpolate(table, position, bins):
    low = jnp.floor(position)
    first = low.astype(jnp.int32)
    second = jnp.minimum(first + 1, bins - 1)
    low_weight = rounded(1.0 - jnp.abs(position - low))
    high_weight = rounded(jnp.maximum(0.0, 1.0 - jnp.abs(position - (low + 1.0))))
    return low_weight * gather_lanes(table, first) + high_weight * gather_lanes(table, second)


def own_fit_rows(live_ref, day_ref, date_slots, dates, first_date):
    size = max(dates, SUBLANES)
    rows, cols = iota((size, size), 0), iota((size, size), 1)

    def place(t, carry):
        day_r, day_c, live_r, live_c = carry
        day = day_ref[t]
        live = (lax.rem(t, date_slots) < live_ref[lax.div(t, date_slots)]).astype(jnp.int32)
        return (
            jnp.where(rows == t, day, day_r),
            jnp.where(cols == t, day, day_c),
            jnp.where(rows == t, live, live_r),
            jnp.where(cols == t, live, live_c),
        )

    zero = jnp.zeros((size, size), jnp.int32)
    day_r, day_c, live_r, live_c = lax.fori_loop(
        0, dates, place, (zero, zero, zero, zero), unroll=dates <= 16
    )
    base = jnp.cos((2.0 * math.pi / YEAR) * (day_r - day_c).astype(jnp.float32))
    older, newer = jnp.ones_like(base), base
    total = older + newer
    for _ in range(HARMONICS - 1):
        older, newer = newer, 2.0 * base * newer - older
        total = total + newer
    eye = jnp.where(rows == cols, 1.0, 0.0)
    work = jnp.where((live_r * live_c) == 1, total, 0.0) + RIDGE * eye
    inverse = eye
    for k in range(dates):
        pivot = work[k : k + 1, k : k + 1]
        row_w, row_i = work[k : k + 1, :] / pivot, inverse[k : k + 1, :] / pivot
        column = work[:, k : k + 1]
        work = jnp.where(rows == k, row_w, work - column * row_w)
        inverse = jnp.where(rows == k, row_i, inverse - column * row_i)
    return [
        jnp.sum(jnp.where(rows == first_date + d, inverse, 0.0), axis=0, keepdims=True)
        for d in range(date_slots)
    ]


def kernel(
    groups,
    spaces,
    live_ref,
    day_ref,
    reflect_ref,
    clear_ref,
    quantile_ref,
    out_ref,
    padded,
    quant,
    hist_own,
    hist_all,
    mask_all,
    series_all,
    hist_send,
    hist_recv,
    mask_send,
    mask_recv,
    series_send,
    series_recv,
):
    date_slots, bands, pixels = reflect_ref.shape
    bins = quantile_ref.shape[1]
    dates = date_slots * groups
    my_date, my_space = lax.axis_index("date"), lax.axis_index("space")
    date_peers = [lax.rem(my_date + i, groups) for i in range(1, groups)]
    space_peers = [lax.rem(my_space + i, spaces) for i in range(1, spaces)]

    barrier = pltpu.get_barrier_semaphore()
    for peer in space_peers:
        pl.semaphore_signal(barrier, inc=1, device_id={"space": peer}, device_id_type=MESH)
    for peer in date_peers:
        pl.semaphore_signal(barrier, inc=1, device_id={"date": peer}, device_id_type=MESH)

    padded[...] = jnp.zeros_like(padded)
    padded[:, :bands] = reflect_ref[...]
    quant[...] = jnp.zeros_like(quant)
    quant[:bands] = rounded(quantile_ref[...])

    inner, spill = [], []
    for d in range(date_slots):
        live = lax.rem(jnp.int32(d), date_slots) < live_ref[my_date]
        valid = clear_ref[d : d + 1, :] * live.astype(jnp.int32)
        mask_all[my_date, d : d + 1, :] = valid.astype(jnp.float32)
        block, extra = block_histogram(
            padded[d], jnp.broadcast_to(valid, (SUBLANES, pixels)) == 1, bands, bins
        )
        inner.append(block)
        spill.append(extra)
    sums = running_sums(inner, spill, bands, bins)
    for d in range(date_slots):
        hist_own[d] = sums[d]

    pl.semaphore_wait(barrier, groups + spaces - 2)

    copies = []
    for peer in space_peers:
        copy = pltpu.make_async_remote_copy(
            src_ref=hist_own,
            dst_ref=hist_all.at[my_space],
            send_sem=hist_send.at[peer],
            recv_sem=hist_recv.at[my_space],
            device_id={"space": peer},
            device_id_type=MESH,
        )
        copy.start()
        copies.append(copy)
    for peer in date_peers:
        copy = pltpu.make_async_remote_copy(
            src_ref=mask_all.at[my_date],
            dst_ref=mask_all.at[my_date],
            send_sem=mask_send.at[peer],
            recv_sem=mask_recv.at[my_date],
            device_id={"date": peer},
            device_id_type=MESH,
        )
        copy.start()
        copies.append(copy)

    fit_rows = own_fit_rows(live_ref, day_ref, date_slots, dates, my_date * date_slots)

    total = [hist_own[d] for d in range(date_slots)]
    for peer in space_peers:
        pltpu.make_async_remote_copy(
            src_ref=hist_own,
            dst_ref=hist_all.at[peer],
            send_sem=hist_send.at[peer],
            recv_sem=hist_recv.at[peer],
            device_id={"space": peer},
            device_id_type=MESH,
        ).wait_recv()
        for d in range(date_slots):
            total[d] = total[d] + hist_all[peer, d]

    for d in range(date_slots):
        table = flat_table(total[d], bands, bins)
        for start in range(0, pixels, LANES):
            span = slice(start, start + LANES)
            position = jnp.clip(bins * padded[d, :, span] - 0.5, 0.0, bins - 1.0)
            level = interpolate(table, position, bins)
            level = jnp.clip(bins * level - 0.5, 0.0, bins - 1.0)
            matched = interpolate(quant[...], level, bins)
            series_all[my_date, d, :, span] = matched[:bands] * mask_all[my_date, d : d + 1, span]
        for peer in date_peers:
            copy = pltpu.make_async_remote_copy(
                src_ref=series_all.at[my_date, d],
                dst_ref=series_all.at[my_date, d],
                send_sem=series_send.at[peer, d],
                recv_sem=series_recv.at[my_date, d],
                device_id={"date": peer},
                device_id_type=MESH,
            )
            copy.start()
            copies.append(copy)

    for peer in date_peers:
        pltpu.make_async_remote_copy(
            src_ref=mask_all.at[peer],
            dst_ref=mask_all.at[peer],
            send_sem=mask_send.at[peer],
            recv_sem=mask_recv.at[peer],
            device_id={"date": peer},
            device_id_type=MESH,
        ).wait_recv()
    for d in range(date_slots):
        for peer in date_peers:
            pltpu.make_async_remote_copy(
                src_ref=series_all.at[peer, d],
                dst_ref=series_all.at[peer, d],
                send_sem=series_send.at[peer, d],
                recv_sem=series_recv.at[peer, d],
                device_id={"date": peer},
                device_id_type=MESH,
            ).wait_recv()

    count = jnp.zeros((1, pixels), jnp.float32)
    summed = jnp.zeros((bands, pixels), jnp.float32)
    gaps = [jnp.zeros((1, pixels), jnp.float32) for _ in range(date_slots)]
    fits = [jnp.zeros((bands, pixels), jnp.float32) for _ in range(date_slots)]
    for t in range(dates):
        g, s = divmod(t, date_slots)
        mask, series = mask_all[g, s : s + 1, :], series_all[g, s]
        count += mask
        summed += series
        for d in range(date_slots):
            weight = fit_rows[d][:, t : t + 1]
            gaps[d] += weight * (1.0 - mask)
            fits[d] += weight * series
    mean = summed / jnp.maximum(count, 1.0)
    for d in range(date_slots):
        out_ref[d] = mask_all[my_date, d : d + 1, :] * (fits[d] + gaps[d] * mean)

    for copy in copies:
        copy.wait_send()


def per_device(groups, spaces, reflect, clear_sky, live_dates, day_of_year, ref_quantile):
    date_slots, bands, pixels = reflect.shape
    bins = ref_quantile.shape[1]
    vmem, smem = pl.BlockSpec(memory_space=pltpu.VMEM), pl.BlockSpec(memory_space=pltpu.SMEM)
    return pl.pallas_call(
        functools.partial(kernel, groups, spaces),
        out_shape=jax.ShapeDtypeStruct(reflect.shape, jnp.float32),
        in_specs=[smem, smem, vmem, vmem, vmem],
        out_specs=vmem,
        scratch_shapes=[
            pltpu.VMEM((date_slots, SUBLANES, pixels), jnp.float32),
            pltpu.VMEM((SUBLANES, bins), jnp.float32),
            pltpu.VMEM((date_slots, LOW, LANES), jnp.float32),
            pltpu.VMEM((spaces, date_slots, LOW, LANES), jnp.float32),
            pltpu.VMEM((groups, date_slots, pixels), jnp.float32),
            pltpu.VMEM((groups, date_slots, bands, pixels), jnp.float32),
            pltpu.SemaphoreType.DMA((spaces,)),
            pltpu.SemaphoreType.DMA((spaces,)),
            pltpu.SemaphoreType.DMA((groups,)),
            pltpu.SemaphoreType.DMA((groups,)),
            pltpu.SemaphoreType.DMA((groups, date_slots)),
            pltpu.SemaphoreType.DMA((groups, date_slots)),
        ],
        compiler_params=pltpu.CompilerParams(collective_id=0, has_side_effects=True),
    )(live_dates, day_of_year, reflect, clear_sky, ref_quantile)


def solution(mesh):
    return jax.shard_map(
        functools.partial(per_device, mesh.shape["date"], mesh.shape["space"]),
        mesh=mesh,
        in_specs=(
            P("date", None, ("tiles", "space")),
            P("date", ("tiles", "space")),
            P(),
            P(),
            P(),
        ),
        out_specs=P("date", None, ("tiles", "space")),
        check_vma=False,
    )
```

time: 67.5 us -> 20.6 us (0.31)
  blocking collectives: 19.8 us -> 0 us
  Pallas kernels: 0 us -> 17.4 us
  other arithmetic: 14.2 us -> 0 us
  starting transfers between devices: 11.1 us -> 0 us
  matrix products: 8.85 us -> 0 us
  local copies, waits for them, and re-layouts: 11.1 us -> 2.93 us
  waiting for transfers between devices: 1.44 us -> 0 us
    pallas_call x0 -> x1, Pallas kernels: none -> 17.4 us  [per_device(): pl.pallas_call(functools.partial(kernel, groups, spaces), out_shape=jax.S...]
    all_to_all x2 -> x0, starting transfers between devices: 11.1 us -> none  [the longest x1 6.32 us: per_device(): lax.all_to_all(valid_mask[:, None, :], 'date', split_axis=2, concat_axis=...]
    psum x1 -> x0, blocking collectives: 10.6 us -> none  [per_device(): histogram = lax.psum(histogram, 'space')]
    all_to_all x1 -> x0, blocking collectives: 9.21 us -> none  [per_device(): lax.all_to_all(leftover, 'date', split_axis=0, concat_axis=2, tiled=True)]
    dot_general x15 -> x0, matrix products: 8.53 us -> none  [the longest x4 2.66 us: add_block(): jnp.einsum('dbpk,dp->dbk', weights, mask_part, preferred_element_type=jnp...]
    another operation x8 -> x0, other arithmetic: 7.65 us -> none
    unnamed x14 -> x1, local copies, waits for them, and re-layouts: 7.1 us -> 1.43 us
    reduce_sum x4 -> x0, other arithmetic: 2.29 us -> none  [the longest x2 2.18 us: per_device(): valid_count = jnp.sum(mask_float, axis=0)]
  transfers between devices with their start and end apart: 2 -> 0, of which waited for: 1 -> 0; matrix products, arithmetic and copies ran while one was open for 36% -> 0% of each run, Pallas kernels for 0% -> 0%
where the time goes in v1:
time: 20.6 us; the launch traced here: 20.3 us
  Pallas kernels  17.4 us (84%)
  local copies, waits for them, and re-layouts  2.93 us (14%)
    pallas_call x1, Pallas kernels, per_device(): pl.pallas_call(functools.partial(kernel, groups, spaces), out_shape=jax.S...  17.4 us
    pallas_call x1, local copies, waits for them, and re-layouts, per_device(): pl.pallas_call(functools.partial(kernel, groups, spaces), out_shape=jax.S...  1.5 us
    unnamed x1, local copies, waits for them, and re-layouts  1.43 us

profile of v1, /device:TPU:0, one launch (start us, length us, event | category | flops | bytes accessed | tf_op | source)
XLA Modules:
  0.0 20.3 jit_solution(14957370361795427837)
XLA Ops:
  0.0 1.4 %copy.6.reflect_ref = f32[2,6,1024]{2,1,0:T(8,128)} copy(f32[2,6,1024]{2,0,1:T(2,128)} %param.5) | data formatting | bytes 98304 | tf_op args[0]
  1.4 17.4 %shard_map.55 = f32[2,6,1024]{2,1,0:T(8,128)} custom-call(s32[4]{0:T(128)} %live_ref.1, s32[8]{0:T(128)} %day_ref.1, f32[2,6,1024]{2,1,0:T(8,128)} %copy.6.reflect_ref, s32[2,1024]{1,0:T(2,128)} %clear_ref.1, f32[6,256]{1,0:T(8,128)} %quantile_ref.1), custom_call_target="tpu_custom_call" | custom-call | tf_op jit(solution)/shard_map/pallas_call | solution.py:344
  18.8 1.5 %copy.7 = f32[2,6,1024]{2,0,1:T(2,128)} copy(f32[2,6,1024]{2,1,0:T(8,128)} %shard_map.55) | data formatting | bytes 98304 | tf_op jit(solution)/shard_map/pallas_call | solution.py:344

commit v2 on v1

--- a/solution.py
+++ b/solution.py
@@ -183,12 +183,18 @@
 def kernel(
     groups,
     spaces,
+    live_hbm,
+    day_hbm,
+    reflect_hbm,
+    clear_hbm,
+    quantile_hbm,
+    out_ref,
     live_ref,
     day_ref,
     reflect_ref,
     clear_ref,
     quantile_ref,
-    out_ref,
+    in_sems,
     padded,
     quant,
     hist_own,
@@ -202,7 +208,7 @@
     series_send,
     series_recv,
 ):
-    date_slots, bands, pixels = reflect_ref.shape
+    bands, date_slots, pixels = reflect_ref.shape
     bins = quantile_ref.shape[1]
     dates = date_slots * groups
     my_date, my_space = lax.axis_index("date"), lax.axis_index("space")
@@ -215,9 +221,27 @@
     for peer in date_peers:
         pl.semaphore_signal(barrier, inc=1, device_id={"date": peer}, device_id_type=MESH)
 
+    loads = [
+        pltpu.make_async_copy(src, dst, in_sems.at[i])
+        for i, (src, dst) in enumerate(
+            (
+                (reflect_hbm, reflect_ref),
+                (clear_hbm, clear_ref),
+                (live_hbm, live_ref),
+                (day_hbm, day_ref),
+                (quantile_hbm, quantile_ref),
+            )
+        )
+    ]
+    for load in loads:
+        load.start()
     padded[...] = jnp.zeros_like(padded)
-    padded[:, :bands] = reflect_ref[...]
     quant[...] = jnp.zeros_like(quant)
+    for load in loads:
+        load.wait()
+    for b in range(bands):
+        for d in range(date_slots):
+            padded[d, b : b + 1, :] = reflect_ref[b, d : d + 1, :]
     quant[:bands] = rounded(quantile_ref[...])
 
     inner, spill = [], []
@@ -259,8 +283,6 @@
         )
         copy.start()
         copies.append(copy)
-
-    fit_rows = own_fit_rows(live_ref, day_ref, date_slots, dates, my_date * date_slots)
 
     total = [hist_own[d] for d in range(date_slots)]
     for peer in space_peers:
@@ -296,6 +318,8 @@
             copy.start()
             copies.append(copy)
 
+    fit_rows = own_fit_rows(live_ref, day_ref, date_slots, dates, my_date * date_slots)
+
     for peer in date_peers:
         pltpu.make_async_remote_copy(
             src_ref=mask_all.at[peer],
@@ -331,7 +355,9 @@
             fits[d] += weight * series
     mean = summed / jnp.maximum(count, 1.0)
     for d in range(date_slots):
-        out_ref[d] = mask_all[my_date, d : d + 1, :] * (fits[d] + gaps[d] * mean)
+        left = mask_all[my_date, d : d + 1, :] * (fits[d] + gaps[d] * mean)
+        for b in range(bands):
+            out_ref[b, d : d + 1, :] = left[b : b + 1]
 
     for copy in copies:
         copy.wait_send()
@@ -340,13 +366,19 @@
 def per_device(groups, spaces, reflect, clear_sky, live_dates, day_of_year, ref_quantile):
     date_slots, bands, pixels = reflect.shape
     bins = ref_quantile.shape[1]
-    vmem, smem = pl.BlockSpec(memory_space=pltpu.VMEM), pl.BlockSpec(memory_space=pltpu.SMEM)
-    return pl.pallas_call(
+    by_band = jnp.transpose(reflect, (1, 0, 2))
+    residual = pl.pallas_call(
         functools.partial(kernel, groups, spaces),
-        out_shape=jax.ShapeDtypeStruct(reflect.shape, jnp.float32),
-        in_specs=[smem, smem, vmem, vmem, vmem],
-        out_specs=vmem,
+        out_shape=jax.ShapeDtypeStruct(by_band.shape, jnp.float32),
+        in_specs=[pl.BlockSpec(memory_space=pl.ANY)] * 5,
+        out_specs=pl.BlockSpec(memory_space=pltpu.VMEM),
         scratch_shapes=[
+            pltpu.SMEM(live_dates.shape, jnp.int32),
+            pltpu.SMEM(day_of_year.shape, jnp.int32),
+            pltpu.VMEM(by_band.shape, jnp.float32),
+            pltpu.VMEM(clear_sky.shape, jnp.int32),
+            pltpu.VMEM(ref_quantile.shape, jnp.float32),
+            pltpu.SemaphoreType.DMA((5,)),
             pltpu.VMEM((date_slots, SUBLANES, pixels), jnp.float32),
             pltpu.VMEM((SUBLANES, bins), jnp.float32),
             pltpu.VMEM((date_slots, LOW, LANES), jnp.float32),
@@ -361,7 +393,8 @@
             pltpu.SemaphoreType.DMA((groups, date_slots)),
         ],
         compiler_params=pltpu.CompilerParams(collective_id=0, has_side_effects=True),
-    )(live_dates, day_of_year, reflect, clear_sky, ref_quantile)
+    )(live_dates, day_of_year, by_band, clear_sky, ref_quantile)
+    return jnp.transpose(residual, (1, 0, 2))
 
 
 def solution(mesh):

time: 20.6 us -> 18.5 us (0.90)
  local copies, waits for them, and re-layouts: 2.93 us -> 1.42 us
  Pallas kernels: 17.4 us -> 16.9 us
    pallas_call x1 -> x0, local copies, waits for them, and re-layouts: 1.5 us -> none  [per_device(): pl.pallas_call(functools.partial(kernel, groups, spaces), out_shape=jax.S...]
    pallas_call x1, Pallas kernels: 17.4 us -> 16.9 us  [per_device(): pl.pallas_call(functools.partial(kernel, groups, spaces), out_shape=jax.S...]
where the time goes in v2:
time: 18.5 us; the launch traced here: 18.3 us
  Pallas kernels  16.9 us (91%)
  local copies, waits for them, and re-layouts  1.42 us (8%)
    pallas_call x1, Pallas kernels, per_device(): pl.pallas_call(functools.partial(kernel, groups, spaces), out_shape=jax.S...  16.9 us
    unnamed x1, local copies, waits for them, and re-layouts  1.42 us

profile of v2, /device:TPU:0, one launch (start us, length us, event | category | flops | bytes accessed | tf_op | source)
XLA Modules:
  0.0 18.3 jit_solution(16486619685064268980)
XLA Ops:
  0.0 16.9 %shard_map.55 = f32[6,2,1024]{2,1,0:T(2,128)} custom-call(s32[4]{0:T(128)} %live_hbm.1, s32[8]{0:T(128)} %day_hbm.1, f32[6,2,1024]{2,1,0:T(2,128)} %bitcast.3, s32[2,1024]{1,0:T(2,128)} %clear_hbm.1, f32[6,256]{1,0:T(8,128)} %quantile_hbm.1), custom_call_target="tpu_custom_call" | custom-call | tf_op jit(solution)/shard_map/pallas_call | solution.py:370
  16.9 1.4 %copy.7 = f32[2,6,1024]{2,0,1:T(2,128)} copy(f32[2,6,1024]{2,0,1:T(2,128)} %bitcast.2) | data formatting | bytes 98304

commit v3 on v2

--- a/solution.py
+++ b/solution.py
@@ -370,7 +370,7 @@
     residual = pl.pallas_call(
         functools.partial(kernel, groups, spaces),
         out_shape=jax.ShapeDtypeStruct(by_band.shape, jnp.float32),
-        in_specs=[pl.BlockSpec(memory_space=pl.ANY)] * 5,
+        in_specs=[pl.BlockSpec(memory_space=pltpu.HBM)] * 5,
         out_specs=pl.BlockSpec(memory_space=pltpu.VMEM),
         scratch_shapes=[
             pltpu.SMEM(live_dates.shape, jnp.int32),
@@ -392,7 +392,9 @@
             pltpu.SemaphoreType.DMA((groups, date_slots)),
             pltpu.SemaphoreType.DMA((groups, date_slots)),
         ],
-        compiler_params=pltpu.CompilerParams(collective_id=0, has_side_effects=True),
+        compiler_params=pltpu.CompilerParams(
+            collective_id=0, has_side_effects=True, vmem_limit_bytes=16 * 2**20
+        ),
     )(live_dates, day_of_year, by_band, clear_sky, ref_quantile)
     return jnp.transpose(residual, (1, 0, 2))
 

time: 18.5 us -> 20 us (1.081)
  local copies, waits for them, and re-layouts: 1.42 us -> 3.48 us
  Pallas kernels: 16.9 us -> 16.2 us
    unnamed x1 -> x11, local copies, waits for them, and re-layouts: 1.42 us -> 3.48 us
    pallas_call x1, Pallas kernels: 16.9 us -> 16.2 us  [per_device(): pl.pallas_call(functools.partial(kernel, groups, spaces), out_shape=jax.S...]
where the time goes in v3:
time: 20 us; the launch traced here: 19.7 us
  Pallas kernels  16.2 us (81%)
  local copies, waits for them, and re-layouts  3.48 us (17%)
    pallas_call x1, Pallas kernels, per_device(): pl.pallas_call(functools.partial(kernel, groups, spaces), out_shape=jax.S...  16.2 us
    unnamed x11, local copies, waits for them, and re-layouts  3.48 us

profile of v3, /device:TPU:0, one launch (start us, length us, event | category | flops | bytes accessed | tf_op | source)
XLA Modules:
  0.0 19.7 jit_solution(11664009243120403766)
XLA Ops:
  0.0 0.0 copy-start.4
  0.0 0.0 copy-start.3
  0.0 0.7 %copy-done.4 = s32[8]{0:T(128)S(1)} copy-done((s32[8]{0:T(128)S(1)}, s32[8]{0:T(128)}, u32[]{:S(2)}) %copy-start.4) | copy-done | bytes 56
  0.7 0.0 copy-done.3
  0.7 0.0 copy-start
  0.7 0.8 %copy-done = f32[2,6,1024]{2,0,1:T(2,128)S(1)} copy-done((f32[2,6,1024]{2,0,1:T(2,128)S(1)}, f32[2,6,1024]{2,0,1:T(2,128)}, u32[]{:S(2)}) %copy-start) | copy-done | bytes 49176
  1.5 0.0 copy-start.1
  1.5 0.7 %copy-done.1 = s32[2,1024]{1,0:T(2,128)S(1)} copy-done((s32[2,1024]{1,0:T(2,128)S(1)}, s32[2,1024]{1,0:T(2,128)}, u32[]{:S(2)}) %copy-start.1) | copy-done | bytes 8216
  2.2 0.0 copy-start.2
  2.2 0.7 %copy-done.2 = f32[6,256]{1,0:T(8,128)S(1)} copy-done((f32[6,256]{1,0:T(8,128)S(1)}, f32[6,256]{1,0:T(8,128)}, u32[]{:S(2)}) %copy-start.2) | copy-done | bytes 6168
  2.9 16.2 %shard_map.55 = f32[6,2,1024]{2,1,0:T(2,128)S(1)} custom-call(s32[4]{0:T(128)S(1)} %copy-done.3, s32[8]{0:T(128)S(1)} %copy-done.4, f32[6,2,1024]{2,1,0:T(2,128)S(1)} %bitcast.3, s32[2,1024]{1,0:T(2,128)S(1)} %copy-done.1, f32[6,256]{1,0:T(8,128)S(1)} %copy-done.2), custom_call_target="tpu_custom_call" | custom-call | tf_op jit(solution)/shard_map/pallas_call | solution.py:370
  19.1 0.6 %copy.7 = f32[2,6,1024]{2,0,1:T(2,128)} copy(f32[2,6,1024]{2,0,1:T(2,128)S(1)} %bitcast.2) | data formatting | bytes 98304
Async XLA Ops:
  0.0 0.7 %copy-start.4 = (s32[8]{0:T(128)S(1)}, s32[8]{0:T(128)}, u32[]{:S(2)}) copy-start(s32[8]{0:T(128)} %day_hbm.1) | copy-start | bytes 100
  0.0 0.7 %copy-start.3 = (s32[4]{0:T(128)S(1)}, s32[4]{0:T(128)}, u32[]{:S(2)}) copy-start(s32[4]{0:T(128)} %live_hbm.1) | copy-start | bytes 52
  0.7 0.8 %copy-start = (f32[2,6,1024]{2,0,1:T(2,128)S(1)}, f32[2,6,1024]{2,0,1:T(2,128)}, u32[]{:S(2)}) copy-start(f32[2,6,1024]{2,0,1:T(2,128)} %param.5) | copy-start | bytes 147460
  1.5 0.7 %copy-start.1 = (s32[2,1024]{1,0:T(2,128)S(1)}, s32[2,1024]{1,0:T(2,128)}, u32[]{:S(2)}) copy-start(s32[2,1024]{1,0:T(2,128)} %clear_hbm.1) | copy-start | bytes 24580
  2.2 0.7 %copy-start.2 = (f32[6,256]{1,0:T(8,128)S(1)}, f32[6,256]{1,0:T(8,128)}, u32[]{:S(2)}) copy-start(f32[6,256]{1,0:T(8,128)} %quantile_hbm.1) | copy-start | bytes 18436

commit v4 on v3

--- a/solution.py
+++ b/solution.py
@@ -395,7 +395,12 @@
         compiler_params=pltpu.CompilerParams(
             collective_id=0, has_side_effects=True, vmem_limit_bytes=16 * 2**20
         ),
-    )(live_dates, day_of_year, by_band, clear_sky, ref_quantile)
+    )(
+        *(
+            pltpu.with_memory_space_constraint(x, pltpu.HBM)
+            for x in (live_dates, day_of_year, by_band, clear_sky, ref_quantile)
+        )
+    )
     return jnp.transpose(residual, (1, 0, 2))
 
 

time: 20 us -> 17 us (0.85)
  local copies, waits for them, and re-layouts: 3.48 us -> 0.62 us
    unnamed x11 -> x1, local copies, waits for them, and re-layouts: 3.48 us -> 0.62 us
where the time goes in v4:
time: 17 us; the launch traced here: 16.9 us
  Pallas kernels  16.2 us (95%)
  local copies, waits for them, and re-layouts  0.62 us (4%)
    pallas_call x1, Pallas kernels, per_device(): pl.pallas_call(functools.partial(kernel, groups, spaces), out_shape=jax.S...  16.2 us
    unnamed x1, local copies, waits for them, and re-layouts  0.62 us

profile of v4, /device:TPU:0, one launch (start us, length us, event | category | flops | bytes accessed | tf_op | source)
XLA Modules:
  0.0 16.9 jit_solution(11293412466843537838)
XLA Ops:
  0.0 16.2 %shard_map.55 = f32[6,2,1024]{2,1,0:T(2,128)S(1)} custom-call(s32[4]{0:T(128)} %live_hbm.1, s32[8]{0:T(128)} %day_hbm.1, f32[6,2,1024]{2,1,0:T(2,128)} %bitcast.3, s32[2,1024]{1,0:T(2,128)} %clear_hbm.1, f32[6,256]{1,0:T(8,128)} %quantile_hbm.1), custom_call_target="tpu_custom_call" | custom-call | tf_op jit(solution)/shard_map/pallas_call | solution.py:370
  16.2 0.6 %copy.7 = f32[2,6,1024]{2,0,1:T(2,128)} copy(f32[2,6,1024]{2,0,1:T(2,128)S(1)} %bitcast.2) | data formatting | bytes 98304

commit v5 on v4

--- a/solution.py
+++ b/solution.py
@@ -183,6 +183,7 @@
 def kernel(
     groups,
     spaces,
+    early,
     live_hbm,
     day_hbm,
     reflect_hbm,
@@ -200,26 +201,80 @@
     hist_own,
     hist_all,
     mask_all,
-    series_all,
+    raw_all,
+    table_all,
+    early_all,
+    late_all,
     hist_send,
     hist_recv,
     mask_send,
     mask_recv,
-    series_send,
-    series_recv,
+    raw_send,
+    raw_recv,
+    table_send,
+    table_recv,
+    late_send,
+    late_recv,
 ):
     bands, date_slots, pixels = reflect_ref.shape
     bins = quantile_ref.shape[1]
     dates = date_slots * groups
     my_date, my_space = lax.axis_index("date"), lax.axis_index("space")
-    date_peers = [lax.rem(my_date + i, groups) for i in range(1, groups)]
     space_peers = [lax.rem(my_space + i, spaces) for i in range(1, spaces)]
+
+    def each_date_peer(body):
+        def step(i, carry):
+            body(lax.rem(my_date + i, groups))
+            return carry
+
+        if groups <= 8:
+            for i in range(1, groups):
+                step(i, 0)
+        else:
+            lax.fori_loop(1, groups, step, 0)
+
+    def to_date(src, dst, send, recv, peer):
+        return pltpu.make_async_remote_copy(
+            src_ref=src,
+            dst_ref=dst,
+            send_sem=send,
+            recv_sem=recv,
+            device_id={"date": peer},
+            device_id_type=MESH,
+        )
+
+    def mask_copy(peer, slot):
+        return to_date(
+            mask_all.at[slot], mask_all.at[slot], mask_send.at[peer], mask_recv.at[slot], peer
+        )
+
+    def raw_copy(peer, slot):
+        return to_date(
+            raw_all.at[slot], raw_all.at[slot], raw_send.at[peer], raw_recv.at[slot], peer
+        )
+
+    def table_copy(peer, slot):
+        return to_date(
+            table_all.at[slot], table_all.at[slot], table_send.at[peer], table_recv.at[slot], peer
+        )
+
+    def late_copy(peer, slot, d):
+        return to_date(
+            late_all.at[slot, d],
+            late_all.at[slot, d],
+            late_send.at[peer, d],
+            late_recv.at[slot, d],
+            peer,
+        )
 
     barrier = pltpu.get_barrier_semaphore()
     for peer in space_peers:
         pl.semaphore_signal(barrier, inc=1, device_id={"space": peer}, device_id_type=MESH)
-    for peer in date_peers:
-        pl.semaphore_signal(barrier, inc=1, device_id={"date": peer}, device_id_type=MESH)
+    each_date_peer(
+        lambda peer: pl.semaphore_signal(
+            barrier, inc=1, device_id={"date": peer}, device_id_type=MESH
+        )
+    )
 
     loads = [
         pltpu.make_async_copy(src, dst, in_sems.at[i])
@@ -241,7 +296,10 @@
         load.wait()
     for b in range(bands):
         for d in range(date_slots):
-            padded[d, b : b + 1, :] = reflect_ref[b, d : d + 1, :]
+            row = reflect_ref[b, d : d + 1, :]
+            padded[d, b : b + 1, :] = row
+            if d < early:
+                raw_all[my_date, d, b : b + 1, :] = row
     quant[:bands] = rounded(quantile_ref[...])
 
     inner, spill = [], []
@@ -260,7 +318,7 @@
 
     pl.semaphore_wait(barrier, groups + spaces - 2)
 
-    copies = []
+    hist_copies = []
     for peer in space_peers:
         copy = pltpu.make_async_remote_copy(
             src_ref=hist_own,
@@ -271,18 +329,9 @@
             device_id_type=MESH,
         )
         copy.start()
-        copies.append(copy)
-    for peer in date_peers:
-        copy = pltpu.make_async_remote_copy(
-            src_ref=mask_all.at[my_date],
-            dst_ref=mask_all.at[my_date],
-            send_sem=mask_send.at[peer],
-            recv_sem=mask_recv.at[my_date],
-            device_id={"date": peer},
-            device_id_type=MESH,
-        )
-        copy.start()
-        copies.append(copy)
+        hist_copies.append(copy)
+    each_date_peer(lambda peer: raw_copy(peer, my_date).start())
+    each_date_peer(lambda peer: mask_copy(peer, my_date).start())
 
     total = [hist_own[d] for d in range(date_slots)]
     for peer in space_peers:
@@ -297,78 +346,100 @@
         for d in range(date_slots):
             total[d] = total[d] + hist_all[peer, d]
 
-    for d in range(date_slots):
-        table = flat_table(total[d], bands, bins)
+    tables = [flat_table(total[d], bands, bins) for d in range(date_slots)]
+    for d in range(early):
+        table_all[my_date, d] = tables[d]
+    each_date_peer(lambda peer: table_copy(peer, my_date).start())
+
+    def match(table, values):
+        position = jnp.clip(bins * values - 0.5, 0.0, bins - 1.0)
+        level = interpolate(table, position, bins)
+        level = jnp.clip(bins * level - 0.5, 0.0, bins - 1.0)
+        return interpolate(quant[...], level, bins)[:bands]
+
+    def match_early(slot):
+        for d in range(early):
+            for start in range(0, pixels, LANES):
+                span = slice(start, start + LANES)
+                matched = match(table_all[slot, d], padded[d, :, span])
+                early_all[slot, d, :, span] = matched * mask_all[slot, d : d + 1, span]
+
+    for d in range(early, date_slots):
         for start in range(0, pixels, LANES):
             span = slice(start, start + LANES)
-            position = jnp.clip(bins * padded[d, :, span] - 0.5, 0.0, bins - 1.0)
-            level = interpolate(table, position, bins)
-            level = jnp.clip(bins * level - 0.5, 0.0, bins - 1.0)
-            matched = interpolate(quant[...], level, bins)
-            series_all[my_date, d, :, span] = matched[:bands] * mask_all[my_date, d : d + 1, span]
-        for peer in date_peers:
-            copy = pltpu.make_async_remote_copy(
-                src_ref=series_all.at[my_date, d],
-                dst_ref=series_all.at[my_date, d],
-                send_sem=series_send.at[peer, d],
-                recv_sem=series_recv.at[my_date, d],
-                device_id={"date": peer},
-                device_id_type=MESH,
-            )
-            copy.start()
-            copies.append(copy)
-
+            matched = match(tables[d], padded[d, :, span])
+            late_all[my_date, d - early, :, span] = matched * mask_all[my_date, d : d + 1, span]
+        each_date_peer(lambda peer: late_copy(peer, my_date, d - early).start())
+
+    match_early(my_date)
     fit_rows = own_fit_rows(live_ref, day_ref, date_slots, dates, my_date * date_slots)
 
-    for peer in date_peers:
-        pltpu.make_async_remote_copy(
-            src_ref=mask_all.at[peer],
-            dst_ref=mask_all.at[peer],
-            send_sem=mask_send.at[peer],
-            recv_sem=mask_recv.at[peer],
-            device_id={"date": peer},
-            device_id_type=MESH,
-        ).wait_recv()
-    for d in range(date_slots):
-        for peer in date_peers:
-            pltpu.make_async_remote_copy(
-                src_ref=series_all.at[peer, d],
-                dst_ref=series_all.at[peer, d],
-                send_sem=series_send.at[peer, d],
-                recv_sem=series_recv.at[peer, d],
-                device_id={"date": peer},
-                device_id_type=MESH,
-            ).wait_recv()
+    def arrived(peer):
+        mask_copy(peer, peer).wait_recv()
+        raw_copy(peer, peer).wait_recv()
+        table_copy(peer, peer).wait_recv()
+        for d in range(early):
+            padded[d, :bands] = raw_all[peer, d]
+        match_early(peer)
+
+    each_date_peer(arrived)
 
     count = jnp.zeros((1, pixels), jnp.float32)
     summed = jnp.zeros((bands, pixels), jnp.float32)
     gaps = [jnp.zeros((1, pixels), jnp.float32) for _ in range(date_slots)]
     fits = [jnp.zeros((bands, pixels), jnp.float32) for _ in range(date_slots)]
-    for t in range(dates):
-        g, s = divmod(t, date_slots)
-        mask, series = mask_all[g, s : s + 1, :], series_all[g, s]
-        count += mask
-        summed += series
-        for d in range(date_slots):
-            weight = fit_rows[d][:, t : t + 1]
-            gaps[d] += weight * (1.0 - mask)
-            fits[d] += weight * series
-    mean = summed / jnp.maximum(count, 1.0)
+    for g in range(groups):
+        for s in range(date_slots):
+            t = g * date_slots + s
+            mask = mask_all[g, s : s + 1, :]
+            count += mask
+            for d in range(date_slots):
+                gaps[d] += fit_rows[d][:, t : t + 1] * (1.0 - mask)
+            if s < early:
+                series = early_all[g, s]
+                summed += series
+                for d in range(date_slots):
+                    fits[d] += fit_rows[d][:, t : t + 1] * series
+    share = 1.0 / jnp.maximum(count, 1.0)
+
+    def late_arrived(peer):
+        for d in range(date_slots - early):
+            late_copy(peer, peer, d).wait_recv()
+
+    each_date_peer(late_arrived)
+    for g in range(groups):
+        for s in range(early, date_slots):
+            t = g * date_slots + s
+            series = late_all[g, s - early]
+            summed += series
+            for d in range(date_slots):
+                fits[d] += fit_rows[d][:, t : t + 1] * series
+    mean = summed * share
     for d in range(date_slots):
         left = mask_all[my_date, d : d + 1, :] * (fits[d] + gaps[d] * mean)
         for b in range(bands):
             out_ref[b, d : d + 1, :] = left[b : b + 1]
 
-    for copy in copies:
+    for copy in hist_copies:
         copy.wait_send()
+
+    def sent(peer):
+        raw_copy(peer, my_date).wait_send()
+        mask_copy(peer, my_date).wait_send()
+        table_copy(peer, my_date).wait_send()
+        for d in range(date_slots - early):
+            late_copy(peer, my_date, d).wait_send()
+
+    each_date_peer(sent)
 
 
 def per_device(groups, spaces, reflect, clear_sky, live_dates, day_of_year, ref_quantile):
     date_slots, bands, pixels = reflect.shape
     bins = ref_quantile.shape[1]
+    early = max(1, date_slots // 2)
     by_band = jnp.transpose(reflect, (1, 0, 2))
     residual = pl.pallas_call(
-        functools.partial(kernel, groups, spaces),
+        functools.partial(kernel, groups, spaces, early),
         out_shape=jax.ShapeDtypeStruct(by_band.shape, jnp.float32),
         in_specs=[pl.BlockSpec(memory_space=pltpu.HBM)] * 5,
         out_specs=pl.BlockSpec(memory_space=pltpu.VMEM),
@@ -384,13 +455,20 @@
             pltpu.VMEM((date_slots, LOW, LANES), jnp.float32),
             pltpu.VMEM((spaces, date_slots, LOW, LANES), jnp.float32),
             pltpu.VMEM((groups, date_slots, pixels), jnp.float32),
-            pltpu.VMEM((groups, date_slots, bands, pixels), jnp.float32),
+            pltpu.VMEM((groups, early, bands, pixels), jnp.float32),
+            pltpu.VMEM((groups, early, SUBLANES, bins), jnp.float32),
+            pltpu.VMEM((groups, early, bands, pixels), jnp.float32),
+            pltpu.VMEM((groups, date_slots - early, bands, pixels), jnp.float32),
             pltpu.SemaphoreType.DMA((spaces,)),
             pltpu.SemaphoreType.DMA((spaces,)),
             pltpu.SemaphoreType.DMA((groups,)),
             pltpu.SemaphoreType.DMA((groups,)),
-            pltpu.SemaphoreType.DMA((groups, date_slots)),
-            pltpu.SemaphoreType.DMA((groups, date_slots)),
+            pltpu.SemaphoreType.DMA((groups,)),
+            pltpu.SemaphoreType.DMA((groups,)),
+            pltpu.SemaphoreType.DMA((groups,)),
+            pltpu.SemaphoreType.DMA((groups,)),
+            pltpu.SemaphoreType.DMA((groups, date_slots - early)),
+            pltpu.SemaphoreType.DMA((groups, date_slots - early)),
         ],
         compiler_params=pltpu.CompilerParams(
             collective_id=0, has_side_effects=True, vmem_limit_bytes=16 * 2**20

time: 17 us -> 14.8 us (0.87)
  Pallas kernels: 16.2 us -> 14 us
    pallas_call x1, Pallas kernels: 16.2 us -> 14 us  [per_device(): pl.pallas_call(functools.partial(kernel, groups, spaces, early), out_shap...]
where the time goes in v5:
time: 14.8 us; the launch traced here: 14.6 us
  Pallas kernels  14 us (95%)
  local copies, waits for them, and re-layouts  0.62 us (4%)
    pallas_call x1, Pallas kernels, per_device(): pl.pallas_call(functools.partial(kernel, groups, spaces, early), out_shap...  14 us
    unnamed x1, local copies, waits for them, and re-layouts  0.62 us

profile of v5, /device:TPU:0, one launch (start us, length us, event | category | flops | bytes accessed | tf_op | source)
XLA Modules:
  0.0 14.6 jit_solution(3248287561074587639)
XLA Ops:
  0.0 14.0 %shard_map.55 = f32[6,2,1024]{2,1,0:T(2,128)S(1)} custom-call(s32[4]{0:T(128)} %live_hbm.1, s32[8]{0:T(128)} %day_hbm.1, f32[6,2,1024]{2,1,0:T(2,128)} %bitcast.3, s32[2,1024]{1,0:T(2,128)} %clear_hbm.1, f32[6,256]{1,0:T(8,128)} %quantile_hbm.1), custom_call_target="tpu_custom_call" | custom-call | tf_op jit(solution)/shard_map/pallas_call | solution.py:441
  14.0 0.6 %copy.7 = f32[2,6,1024]{2,0,1:T(2,128)} copy(f32[2,6,1024]{2,0,1:T(2,128)S(1)} %bitcast.2) | data formatting | bytes 98304

commit v6 on v5

--- a/solution.py
+++ b/solution.py
@@ -23,6 +23,13 @@
 
 def rounded(x):
     return x.astype(jnp.bfloat16).astype(jnp.float32)
+
+
+def three_parts(x):
+    first = x.astype(jnp.bfloat16)
+    rest = x - first.astype(jnp.float32)
+    second = rest.astype(jnp.bfloat16)
+    return first, second, (rest - second.astype(jnp.float32)).astype(jnp.bfloat16)
 
 
 def block_histogram(values, valid, bands, bins):
@@ -74,18 +81,18 @@
     shift = jnp.where(same & (src + 1 == dst), 0.5, 0.0)
     before = jnp.where(src < used, before, 0.0)
     shift = jnp.where(src < used, shift, 0.0)
+    parts = [part.astype(jnp.float32) for part in three_parts(left)] + [jnp.zeros_like(left)]
     moved = jnp.dot(
-        left,
-        jnp.concatenate([before, shift], axis=1),
-        precision=lax.Precision.HIGHEST,
+        jnp.concatenate(parts, axis=0).astype(jnp.bfloat16),
+        jnp.concatenate([before, shift], axis=1).astype(jnp.bfloat16),
         preferred_element_type=jnp.float32,
     )
-    out_row, in_row = iota((LOW, LOW), 0), iota((LOW, LOW), 1)
+    moved = sum(moved[i * SUBLANES : (i + 1) * SUBLANES] for i in range(3))
+    out_row, in_row = iota((LOW, 3 * LOW), 0), iota((LOW, 3 * LOW), 1) % LOW
     lower = jnp.where(in_row < out_row, 1.0, jnp.where(in_row == out_row, 0.5, 0.0))
     within = jnp.dot(
-        lower,
-        jnp.concatenate(inner, axis=1),
-        precision=lax.Precision.HIGHEST,
+        lower.astype(jnp.bfloat16),
+        jnp.concatenate(three_parts(jnp.concatenate(inner, axis=1)), axis=0),
         preferred_element_type=jnp.float32,
     )
     first = iota((LOW, LANES), 0) == 0
@@ -333,6 +340,8 @@
     each_date_peer(lambda peer: raw_copy(peer, my_date).start())
     each_date_peer(lambda peer: mask_copy(peer, my_date).start())
 
+    fit_rows = own_fit_rows(live_ref, day_ref, date_slots, dates, my_date * date_slots)
+
     total = [hist_own[d] for d in range(date_slots)]
     for peer in space_peers:
         pltpu.make_async_remote_copy(
@@ -372,7 +381,6 @@
         each_date_peer(lambda peer: late_copy(peer, my_date, d - early).start())
 
     match_early(my_date)
-    fit_rows = own_fit_rows(live_ref, day_ref, date_slots, dates, my_date * date_slots)
 
     def arrived(peer):
         mask_copy(peer, peer).wait_recv()

time: 14.8 us -> 14.7 us (level)
  no operation moved by 1% of the time
where the time goes in v6:
time: 14.7 us; the launch traced here: 14.6 us
  Pallas kernels  13.9 us (95%)
  local copies, waits for them, and re-layouts  0.62 us (4%)
    pallas_call x1, Pallas kernels, per_device(): pl.pallas_call(functools.partial(kernel, groups, spaces, early), out_shap...  13.9 us
    unnamed x1, local copies, waits for them, and re-layouts  0.62 us

profile of v6, /device:TPU:0, one launch (start us, length us, event | category | flops | bytes accessed | tf_op | source)
XLA Modules:
  0.0 14.6 jit_solution(3593683088702799376)
XLA Ops:
  0.0 13.9 %shard_map.55 = f32[6,2,1024]{2,1,0:T(2,128)S(1)} custom-call(s32[4]{0:T(128)} %live_hbm.1, s32[8]{0:T(128)} %day_hbm.1, f32[6,2,1024]{2,1,0:T(2,128)} %bitcast.3, s32[2,1024]{1,0:T(2,128)} %clear_hbm.1, f32[6,256]{1,0:T(8,128)} %quantile_hbm.1), custom_call_target="tpu_custom_call" | custom-call | tf_op jit(solution)/shard_map/pallas_call | solution.py:449
  13.9 0.6 %copy.7 = f32[2,6,1024]{2,0,1:T(2,128)} copy(f32[2,6,1024]{2,0,1:T(2,128)S(1)} %bitcast.2) | data formatting | bytes 98304

commit v7 on v6

--- a/solution.py
+++ b/solution.py
@@ -32,37 +32,62 @@
     return first, second, (rest - second.astype(jnp.float32)).astype(jnp.bfloat16)
 
 
-def block_histogram(values, valid, bands, bins):
+def row_slot_band(row, bands):
+    whole = SUBLANES - bands
+    slot = (row >= bands).astype(jnp.int32)
+    band = jnp.where(
+        row < bands, row, jnp.where(row < SUBLANES, row - bands + (bands - whole), row - SUBLANES)
+    )
+    return slot, band
+
+
+def find_row(slot, band, bands):
+    rest = 2 * bands - SUBLANES
+    if slot == 0:
+        return 0, band
+    return (1, band) if band < rest else (0, bands + band - rest)
+
+
+def block_histograms(values, valid, bands, bins):
     high_count = bins // LOW
-    pixels = values.shape[1]
-    position = jnp.clip(bins * values - 0.5, 0.0, bins - 1.0)
-    high = jnp.floor(position * (1.0 / LOW))
-    local = position - LOW * high
-    marked = jnp.where(valid, high, -1.0)
+    pixels = values[0].shape[1]
     high_iota = iota((high_count, pixels), 0).astype(jnp.float32)
     low_iota = iota((LOW, pixels), 0).astype(jnp.float32)
-    hot, tents = [], []
-    for b in range(bands):
-        hot.append(jnp.where(high_iota == marked[b : b + 1], 1.0, 0.0).astype(jnp.bfloat16))
-        tents.append(
-            jnp.maximum(0.0, 1.0 - jnp.abs(local[b : b + 1] - low_iota)).astype(jnp.bfloat16)
-        )
-    spill = jnp.maximum(0.0, 1.0 - jnp.abs(local - LOW))
-    tents.append(jnp.concatenate([spill, jnp.zeros_like(spill)], axis=0).astype(jnp.bfloat16))
-    hot.append(jnp.zeros((LANES - bands * high_count, pixels), jnp.bfloat16))
-    counts = lax.dot_general(
-        jnp.concatenate(tents, axis=0),
-        jnp.concatenate(hot, axis=0),
-        (((1,), (1,)), ((), ())),
-        preferred_element_type=jnp.float32,
-    )
+    marked, local, spill = [], [], []
+    for group in range(2):
+        position = jnp.clip(bins * values[group] - 0.5, 0.0, bins - 1.0)
+        high = jnp.floor(position * (1.0 / LOW))
+        local.append(position - LOW * high)
+        marked.append(jnp.where(valid[group] > 0.5, high, -1.0))
+        spill.append(jnp.maximum(0.0, 1.0 - jnp.abs(local[group] - LOW)))
+    spill = jnp.concatenate(spill, axis=0).astype(jnp.bfloat16)
     band_lane = iota((LOW, LANES), 1) // high_count
-    inner = jnp.zeros((LOW, LANES), jnp.float32)
-    for b in range(bands):
-        inner += jnp.where(band_lane == b, counts[b * LOW : (b + 1) * LOW], 0.0)
-    outer = counts[bands * LOW : bands * LOW + SUBLANES]
-    own = iota((SUBLANES, LANES), 0) == band_lane[:SUBLANES]
-    return inner, jnp.sum(jnp.where(own, outer, 0.0), axis=0, keepdims=True)
+    row_slot, row_band = row_slot_band(iota((2 * SUBLANES, LANES), 0), bands)
+    own_lane = iota((2 * SUBLANES, LANES), 1) // high_count
+    inners, outers = [], []
+    for slot in range(2):
+        hot, tents = [], []
+        for band in range(bands):
+            group, row = find_row(slot, band, bands)
+            one = marked[group][row : row + 1]
+            hot.append(jnp.where(high_iota == one, 1.0, 0.0).astype(jnp.bfloat16))
+            near = 1.0 - jnp.abs(local[group][row : row + 1] - low_iota)
+            tents.append(jnp.maximum(0.0, near).astype(jnp.bfloat16))
+        hot.append(jnp.zeros((LANES - bands * high_count, pixels), jnp.bfloat16))
+        counts = lax.dot_general(
+            jnp.concatenate(tents + [spill], axis=0),
+            jnp.concatenate(hot, axis=0),
+            (((1,), (1,)), ((), ())),
+            preferred_element_type=jnp.float32,
+        )
+        inner = jnp.zeros((LOW, LANES), jnp.float32)
+        for band in range(bands):
+            inner += jnp.where(band_lane == band, counts[band * LOW : (band + 1) * LOW], 0.0)
+        own = (row_slot == slot) & (row_band == own_lane)
+        outer = jnp.where(own, counts[bands * LOW : bands * LOW + 2 * SUBLANES], 0.0)
+        inners.append(inner)
+        outers.append(jnp.sum(outer, axis=0, keepdims=True))
+    return inners, outers
 
 
 def running_sums(inner, spill, bands, bins):
@@ -104,28 +129,31 @@
     return sums
 
 
-def flat_table(sums, bands, bins):
+def flat_tables(sums, bands, bins):
     high_count = bins // LOW
     used = bands * high_count
     lane = iota((SUBLANES, LANES), 1)
     total_lane = jnp.minimum(used + lane // high_count, LANES - 1)
-    total = jnp.take_along_axis(sums[:SUBLANES], total_lane, axis=1)[:1]
-    cumulative = (sums / jnp.maximum(total, 1.0)).astype(jnp.bfloat16).astype(jnp.float32)
     band_lane = iota((LOW, LANES), 1) // high_count
-    wide = jnp.concatenate(
-        [jnp.where(band_lane == b, cumulative, 0.0) for b in range(bands)], axis=0
-    ).astype(jnp.bfloat16)
+    wide = []
+    for part in sums:
+        total = jnp.take_along_axis(part[:SUBLANES], total_lane, axis=1)[:1]
+        cumulative = (part / jnp.maximum(total, 1.0)).astype(jnp.bfloat16).astype(jnp.float32)
+        wide += [jnp.where(band_lane == band, cumulative, 0.0) for band in range(bands)]
     src, dst = iota((LANES, bins), 0), iota((LANES, bins), 1)
-    spread = jnp.where((src % high_count == dst // LOW) & (src < used), 1.0, 0.0).astype(
-        jnp.bfloat16
-    )
-    placed = jnp.dot(wide, spread, preferred_element_type=jnp.float32)
+    spread = jnp.where((src % high_count == dst // LOW) & (src < used), 1.0, 0.0)
+    placed = jnp.dot(
+        jnp.concatenate(wide, axis=0).astype(jnp.bfloat16),
+        spread.astype(jnp.bfloat16),
+        preferred_element_type=jnp.float32,
+    )
     rows, cols = iota(placed.shape, 0), iota(placed.shape, 1)
     placed = jnp.where(rows % LOW == cols % LOW, placed, 0.0).astype(jnp.bfloat16)
-    pick = jnp.where(
-        iota((SUBLANES, bands * LOW), 1) // LOW == iota((SUBLANES, bands * LOW), 0), 1.0, 0.0
-    ).astype(jnp.bfloat16)
-    return jnp.dot(pick, placed, preferred_element_type=jnp.float32)
+    shape = (2 * SUBLANES, 2 * bands * LOW)
+    slot, band = row_slot_band(iota(shape, 0), bands)
+    pick = jnp.where((iota(shape, 1) // LOW == slot * bands + band) & (band < bands), 1.0, 0.0)
+    tables = jnp.dot(pick.astype(jnp.bfloat16), placed, preferred_element_type=jnp.float32)
+    return tables[:SUBLANES], tables[SUBLANES:]
 
 
 def gather_lanes(table, index):
@@ -190,7 +218,6 @@
 def kernel(
     groups,
     spaces,
-    early,
     live_hbm,
     day_hbm,
     reflect_hbm,
@@ -203,7 +230,7 @@
     clear_ref,
     quantile_ref,
     in_sems,
-    padded,
+    late_raw,
     quant,
     hist_own,
     hist_all,
@@ -226,6 +253,7 @@
     bands, date_slots, pixels = reflect_ref.shape
     bins = quantile_ref.shape[1]
     dates = date_slots * groups
+    rest = 2 * bands - SUBLANES
     my_date, my_space = lax.axis_index("date"), lax.axis_index("space")
     space_peers = [lax.rem(my_space + i, spaces) for i in range(1, spaces)]
 
@@ -265,13 +293,9 @@
             table_all.at[slot], table_all.at[slot], table_send.at[peer], table_recv.at[slot], peer
         )
 
-    def late_copy(peer, slot, d):
+    def late_copy(peer, slot):
         return to_date(
-            late_all.at[slot, d],
-            late_all.at[slot, d],
-            late_send.at[peer, d],
-            late_recv.at[slot, d],
-            peer,
+            late_all.at[slot], late_all.at[slot], late_send.at[peer], late_recv.at[slot], peer
         )
 
     barrier = pltpu.get_barrier_semaphore()
@@ -297,28 +321,40 @@
     ]
     for load in loads:
         load.start()
-    padded[...] = jnp.zeros_like(padded)
+    late_raw[...] = jnp.zeros_like(late_raw)
     quant[...] = jnp.zeros_like(quant)
     for load in loads:
         load.wait()
-    for b in range(bands):
-        for d in range(date_slots):
-            row = reflect_ref[b, d : d + 1, :]
-            padded[d, b : b + 1, :] = row
-            if d < early:
-                raw_all[my_date, d, b : b + 1, :] = row
-    quant[:bands] = rounded(quantile_ref[...])
-
-    inner, spill = [], []
+    for d in range(date_slots):
+        for b in range(bands):
+            group, row = find_row(d, b, bands)
+            values = reflect_ref[b, d : d + 1, :]
+            if group == 0:
+                raw_all[my_date, row : row + 1, :] = values
+            else:
+                late_raw[row : row + 1, :] = values
+            quant[group, row : row + 1, :] = rounded(quantile_ref[b : b + 1, :])
+
     for d in range(date_slots):
         live = lax.rem(jnp.int32(d), date_slots) < live_ref[my_date]
         valid = clear_ref[d : d + 1, :] * live.astype(jnp.int32)
         mask_all[my_date, d : d + 1, :] = valid.astype(jnp.float32)
-        block, extra = block_histogram(
-            padded[d], jnp.broadcast_to(valid, (SUBLANES, pixels)) == 1, bands, bins
-        )
-        inner.append(block)
-        spill.append(extra)
+
+    def row_mask(slot, span):
+        size = span.stop - span.start
+        slots, _ = row_slot_band(iota((SUBLANES, size), 0), bands)
+        return jnp.where(slots == 0, mask_all[slot, 0:1, span], mask_all[slot, 1:2, span])
+
+    everything = slice(0, pixels)
+    inner, spill = block_histograms(
+        (raw_all[my_date], late_raw[...]),
+        (
+            row_mask(my_date, everything),
+            jnp.broadcast_to(mask_all[my_date, 1:2, :], (SUBLANES, pixels)),
+        ),
+        bands,
+        bins,
+    )
     sums = running_sums(inner, spill, bands, bins)
     for d in range(date_slots):
         hist_own[d] = sums[d]
@@ -355,30 +391,27 @@
         for d in range(date_slots):
             total[d] = total[d] + hist_all[peer, d]
 
-    tables = [flat_table(total[d], bands, bins) for d in range(date_slots)]
-    for d in range(early):
-        table_all[my_date, d] = tables[d]
+    early_table, late_table = flat_tables(total, bands, bins)
+    table_all[my_date] = early_table
     each_date_peer(lambda peer: table_copy(peer, my_date).start())
 
-    def match(table, values):
+    def match(table, values, group):
         position = jnp.clip(bins * values - 0.5, 0.0, bins - 1.0)
         level = interpolate(table, position, bins)
         level = jnp.clip(bins * level - 0.5, 0.0, bins - 1.0)
-        return interpolate(quant[...], level, bins)[:bands]
+        return interpolate(quant[group], level, bins)
 
     def match_early(slot):
-        for d in range(early):
-            for start in range(0, pixels, LANES):
-                span = slice(start, start + LANES)
-                matched = match(table_all[slot, d], padded[d, :, span])
-                early_all[slot, d, :, span] = matched * mask_all[slot, d : d + 1, span]
-
-    for d in range(early, date_slots):
         for start in range(0, pixels, LANES):
             span = slice(start, start + LANES)
-            matched = match(tables[d], padded[d, :, span])
-            late_all[my_date, d - early, :, span] = matched * mask_all[my_date, d : d + 1, span]
-        each_date_peer(lambda peer: late_copy(peer, my_date, d - early).start())
+            matched = match(table_all[slot], raw_all[slot, :, span], 0)
+            early_all[slot, :, span] = matched * row_mask(slot, span)
+
+    for start in range(0, pixels, LANES):
+        span = slice(start, start + LANES)
+        matched = match(late_table, late_raw[:, span], 1)[:rest]
+        late_all[my_date, :, span] = matched * mask_all[my_date, 1:2, span]
+    each_date_peer(lambda peer: late_copy(peer, my_date).start())
 
     match_early(my_date)
 
@@ -386,47 +419,51 @@
         mask_copy(peer, peer).wait_recv()
         raw_copy(peer, peer).wait_recv()
         table_copy(peer, peer).wait_recv()
-        for d in range(early):
-            padded[d, :bands] = raw_all[peer, d]
         match_early(peer)
 
     each_date_peer(arrived)
 
+    row_slot, _ = row_slot_band(iota((SUBLANES, 1), 0), bands)
     count = jnp.zeros((1, pixels), jnp.float32)
-    summed = jnp.zeros((bands, pixels), jnp.float32)
     gaps = [jnp.zeros((1, pixels), jnp.float32) for _ in range(date_slots)]
-    fits = [jnp.zeros((bands, pixels), jnp.float32) for _ in range(date_slots)]
+    summed = jnp.zeros((SUBLANES, pixels), jnp.float32)
+    fits = [jnp.zeros((SUBLANES, pixels), jnp.float32) for _ in range(date_slots)]
     for g in range(groups):
+        series = early_all[g]
+        summed += series
+        for d in range(date_slots):
+            first, second = (fit_rows[d][:, 2 * g + s : 2 * g + s + 1] for s in range(2))
+            fits[d] += jnp.where(row_slot == 0, first, second) * series
         for s in range(date_slots):
-            t = g * date_slots + s
             mask = mask_all[g, s : s + 1, :]
             count += mask
             for d in range(date_slots):
-                gaps[d] += fit_rows[d][:, t : t + 1] * (1.0 - mask)
-            if s < early:
-                series = early_all[g, s]
-                summed += series
-                for d in range(date_slots):
-                    fits[d] += fit_rows[d][:, t : t + 1] * series
+                gaps[d] += fit_rows[d][:, 2 * g + s : 2 * g + s + 1] * (1.0 - mask)
     share = 1.0 / jnp.maximum(count, 1.0)
-
-    def late_arrived(peer):
-        for d in range(date_slots - early):
-            late_copy(peer, peer, d).wait_recv()
-
-    each_date_peer(late_arrived)
+    gaps = [gap * share for gap in gaps]
+
+    def finish(d, row, value):
+        out_ref[row, d : d + 1, :] = value
+
+    for b in range(rest, bands):
+        other = bands + b - rest
+        mean = summed[b : b + 1] + summed[other : other + 1]
+        for d in range(date_slots):
+            fit = fits[d][b : b + 1] + fits[d][other : other + 1] + gaps[d] * mean
+            finish(d, b, mask_all[my_date, d : d + 1, :] * fit)
+
+    each_date_peer(lambda peer: late_copy(peer, peer).wait_recv())
+    summed = summed[:rest]
+    fits = [fit[:rest] for fit in fits]
     for g in range(groups):
-        for s in range(early, date_slots):
-            t = g * date_slots + s
-            series = late_all[g, s - early]
-            summed += series
-            for d in range(date_slots):
-                fits[d] += fit_rows[d][:, t : t + 1] * series
-    mean = summed * share
+        series = late_all[g]
+        summed += series
+        for d in range(date_slots):
+            fits[d] += fit_rows[d][:, 2 * g + 1 : 2 * g + 2] * series
     for d in range(date_slots):
-        left = mask_all[my_date, d : d + 1, :] * (fits[d] + gaps[d] * mean)
-        for b in range(bands):
-            out_ref[b, d : d + 1, :] = left[b : b + 1]
+        left = mask_all[my_date, d : d + 1, :] * (fits[d] + gaps[d] * summed)
+        for b in range(rest):
+            finish(d, b, left[b : b + 1])
 
     for copy in hist_copies:
         copy.wait_send()
@@ -435,8 +472,7 @@
         raw_copy(peer, my_date).wait_send()
         mask_copy(peer, my_date).wait_send()
         table_copy(peer, my_date).wait_send()
-        for d in range(date_slots - early):
-            late_copy(peer, my_date, d).wait_send()
+        late_copy(peer, my_date).wait_send()
 
     each_date_peer(sent)
 
@@ -444,10 +480,10 @@
 def per_device(groups, spaces, reflect, clear_sky, live_dates, day_of_year, ref_quantile):
     date_slots, bands, pixels = reflect.shape
     bins = ref_quantile.shape[1]
-    early = max(1, date_slots // 2)
+    rest = 2 * bands - SUBLANES
     by_band = jnp.transpose(reflect, (1, 0, 2))
     residual = pl.pallas_call(
-        functools.partial(kernel, groups, spaces, early),
+        functools.partial(kernel, groups, spaces),
         out_shape=jax.ShapeDtypeStruct(by_band.shape, jnp.float32),
         in_specs=[pl.BlockSpec(memory_space=pltpu.HBM)] * 5,
         out_specs=pl.BlockSpec(memory_space=pltpu.VMEM),
@@ -458,15 +494,15 @@
             pltpu.VMEM(clear_sky.shape, jnp.int32),
             pltpu.VMEM(ref_quantile.shape, jnp.float32),
             pltpu.SemaphoreType.DMA((5,)),
-            pltpu.VMEM((date_slots, SUBLANES, pixels), jnp.float32),
-            pltpu.VMEM((SUBLANES, bins), jnp.float32),
+            pltpu.VMEM((SUBLANES, pixels), jnp.float32),
+            pltpu.VMEM((2, SUBLANES, bins), jnp.float32),
             pltpu.VMEM((date_slots, LOW, LANES), jnp.float32),
             pltpu.VMEM((spaces, date_slots, LOW, LANES), jnp.float32),
             pltpu.VMEM((groups, date_slots, pixels), jnp.float32),
-            pltpu.VMEM((groups, early, bands, pixels), jnp.float32),
-            pltpu.VMEM((groups, early, SUBLANES, bins), jnp.float32),
-            pltpu.VMEM((groups, early, bands, pixels), jnp.float32),
-            pltpu.VMEM((groups, date_slots - early, bands, pixels), jnp.float32),
+            pltpu.VMEM((groups, SUBLANES, pixels), jnp.float32),
+            pltpu.VMEM((groups, SUBLANES, bins), jnp.float32),
+            pltpu.VMEM((groups, SUBLANES, pixels), jnp.float32),
+            pltpu.VMEM((groups, rest, pixels), jnp.float32),
             pltpu.SemaphoreType.DMA((spaces,)),
             pltpu.SemaphoreType.DMA((spaces,)),
             pltpu.SemaphoreType.DMA((groups,)),
@@ -475,8 +511,8 @@
             pltpu.SemaphoreType.DMA((groups,)),
             pltpu.SemaphoreType.DMA((groups,)),
             pltpu.SemaphoreType.DMA((groups,)),
-            pltpu.SemaphoreType.DMA((groups, date_slots - early)),
-            pltpu.SemaphoreType.DMA((groups, date_slots - early)),
+            pltpu.SemaphoreType.DMA((groups,)),
+            pltpu.SemaphoreType.DMA((groups,)),
         ],
         compiler_params=pltpu.CompilerParams(
             collective_id=0, has_side_effects=True, vmem_limit_bytes=16 * 2**20

time: 14.7 us -> 13.6 us (0.925)
  Pallas kernels: 13.9 us -> 12.8 us
    pallas_call x1, Pallas kernels: 13.9 us -> 12.8 us  [per_device(): pl.pallas_call(functools.partial(kernel, groups, spaces), out_shape=jax.S...]
where the time goes in v7:
time: 13.6 us; the launch traced here: 13.5 us
  Pallas kernels  12.8 us (94%)
  local copies, waits for them, and re-layouts  0.62 us (5%)
    pallas_call x1, Pallas kernels, per_device(): pl.pallas_call(functools.partial(kernel, groups, spaces), out_shape=jax.S...  12.8 us
    unnamed x1, local copies, waits for them, and re-layouts  0.62 us

profile of v7, /device:TPU:0, one launch (start us, length us, event | category | flops | bytes accessed | tf_op | source)
XLA Modules:
  0.0 13.5 jit_solution(1363954701633343774)
XLA Ops:
  0.0 12.8 %shard_map.55 = f32[6,2,1024]{2,1,0:T(2,128)S(1)} custom-call(s32[4]{0:T(128)} %live_hbm.1, s32[8]{0:T(128)} %day_hbm.1, f32[6,2,1024]{2,1,0:T(2,128)} %bitcast.3, s32[2,1024]{1,0:T(2,128)} %clear_hbm.1, f32[6,256]{1,0:T(8,128)} %quantile_hbm.1), custom_call_target="tpu_custom_call" | custom-call | tf_op jit(solution)/shard_map/pallas_call | solution.py:485
  12.9 0.6 %copy.7 = f32[2,6,1024]{2,0,1:T(2,128)} copy(f32[2,6,1024]{2,0,1:T(2,128)S(1)} %bitcast.2) | data formatting | bytes 98304

commit v8 on v7

--- a/solution.py
+++ b/solution.py
@@ -340,6 +340,11 @@
         valid = clear_ref[d : d + 1, :] * live.astype(jnp.int32)
         mask_all[my_date, d : d + 1, :] = valid.astype(jnp.float32)
 
+    pl.semaphore_wait(barrier, groups + spaces - 2)
+
+    each_date_peer(lambda peer: raw_copy(peer, my_date).start())
+    each_date_peer(lambda peer: mask_copy(peer, my_date).start())
+
     def row_mask(slot, span):
         size = span.stop - span.start
         slots, _ = row_slot_band(iota((SUBLANES, size), 0), bands)
@@ -359,8 +364,6 @@
     for d in range(date_slots):
         hist_own[d] = sums[d]
 
-    pl.semaphore_wait(barrier, groups + spaces - 2)
-
     hist_copies = []
     for peer in space_peers:
         copy = pltpu.make_async_remote_copy(
@@ -373,8 +376,6 @@
         )
         copy.start()
         hist_copies.append(copy)
-    each_date_peer(lambda peer: raw_copy(peer, my_date).start())
-    each_date_peer(lambda peer: mask_copy(peer, my_date).start())
 
     fit_rows = own_fit_rows(live_ref, day_ref, date_slots, dates, my_date * date_slots)
 

time: 13.6 us -> 14 us (1.029)
  Pallas kernels: 12.8 us -> 13.2 us
    pallas_call x1, Pallas kernels: 12.8 us -> 13.2 us  [per_device(): pl.pallas_call(functools.partial(kernel, groups, spaces), out_shape=jax.S...]
where the time goes in v8:
time: 14 us; the launch traced here: 13.8 us
  Pallas kernels  13.2 us (94%)
  local copies, waits for them, and re-layouts  0.62 us (4%)
    pallas_call x1, Pallas kernels, per_device(): pl.pallas_call(functools.partial(kernel, groups, spaces), out_shape=jax.S...  13.2 us
    unnamed x1, local copies, waits for them, and re-layouts  0.62 us

profile of v8, /device:TPU:0, one launch (start us, length us, event | category | flops | bytes accessed | tf_op | source)
XLA Modules:
  0.0 13.8 jit_solution(10470414741594872357)
XLA Ops:
  0.0 13.2 %shard_map.55 = f32[6,2,1024]{2,1,0:T(2,128)S(1)} custom-call(s32[4]{0:T(128)} %live_hbm.1, s32[8]{0:T(128)} %day_hbm.1, f32[6,2,1024]{2,1,0:T(2,128)} %bitcast.3, s32[2,1024]{1,0:T(2,128)} %clear_hbm.1, f32[6,256]{1,0:T(8,128)} %quantile_hbm.1), custom_call_target="tpu_custom_call" | custom-call | tf_op jit(solution)/shard_map/pallas_call | solution.py:486
  13.2 0.6 %copy.7 = f32[2,6,1024]{2,0,1:T(2,128)} copy(f32[2,6,1024]{2,0,1:T(2,128)S(1)} %bitcast.2) | data formatting | bytes 98304

commit v9 on v7

--- a/solution.py
+++ b/solution.py
@@ -64,9 +64,8 @@
     band_lane = iota((LOW, LANES), 1) // high_count
     row_slot, row_band = row_slot_band(iota((2 * SUBLANES, LANES), 0), bands)
     own_lane = iota((2 * SUBLANES, LANES), 1) // high_count
-    inners, outers = [], []
+    hot, tents = [], []
     for slot in range(2):
-        hot, tents = [], []
         for band in range(bands):
             group, row = find_row(slot, band, bands)
             one = marked[group][row : row + 1]
@@ -74,17 +73,21 @@
             near = 1.0 - jnp.abs(local[group][row : row + 1] - low_iota)
             tents.append(jnp.maximum(0.0, near).astype(jnp.bfloat16))
         hot.append(jnp.zeros((LANES - bands * high_count, pixels), jnp.bfloat16))
-        counts = lax.dot_general(
-            jnp.concatenate(tents + [spill], axis=0),
-            jnp.concatenate(hot, axis=0),
-            (((1,), (1,)), ((), ())),
-            preferred_element_type=jnp.float32,
-        )
+    counts = lax.dot_general(
+        jnp.concatenate(tents + [spill], axis=0),
+        jnp.concatenate(hot, axis=0),
+        (((1,), (1,)), ((), ())),
+        preferred_element_type=jnp.float32,
+    )
+    inners, outers = [], []
+    for slot in range(2):
+        part = counts[:, slot * LANES : (slot + 1) * LANES]
         inner = jnp.zeros((LOW, LANES), jnp.float32)
         for band in range(bands):
-            inner += jnp.where(band_lane == band, counts[band * LOW : (band + 1) * LOW], 0.0)
+            start = (slot * bands + band) * LOW
+            inner += jnp.where(band_lane == band, part[start : start + LOW], 0.0)
         own = (row_slot == slot) & (row_band == own_lane)
-        outer = jnp.where(own, counts[bands * LOW : bands * LOW + 2 * SUBLANES], 0.0)
+        outer = jnp.where(own, part[2 * bands * LOW :], 0.0)
         inners.append(inner)
         outers.append(jnp.sum(outer, axis=0, keepdims=True))
     return inners, outers
@@ -298,15 +301,6 @@
             late_all.at[slot], late_all.at[slot], late_send.at[peer], late_recv.at[slot], peer
         )
 
-    barrier = pltpu.get_barrier_semaphore()
-    for peer in space_peers:
-        pl.semaphore_signal(barrier, inc=1, device_id={"space": peer}, device_id_type=MESH)
-    each_date_peer(
-        lambda peer: pl.semaphore_signal(
-            barrier, inc=1, device_id={"date": peer}, device_id_type=MESH
-        )
-    )
-
     loads = [
         pltpu.make_async_copy(src, dst, in_sems.at[i])
         for i, (src, dst) in enumerate(
@@ -321,9 +315,18 @@
     ]
     for load in loads:
         load.start()
+
+    barrier = pltpu.get_barrier_semaphore()
+    for peer in space_peers:
+        pl.semaphore_signal(barrier, inc=1, device_id={"space": peer}, device_id_type=MESH)
+    each_date_peer(
+        lambda peer: pl.semaphore_signal(
+            barrier, inc=1, device_id={"date": peer}, device_id_type=MESH
+        )
+    )
+
     late_raw[...] = jnp.zeros_like(late_raw)
-    quant[...] = jnp.zeros_like(quant)
-    for load in loads:
+    for load in loads[:3]:
         load.wait()
     for d in range(date_slots):
         for b in range(bands):
@@ -333,7 +336,6 @@
                 raw_all[my_date, row : row + 1, :] = values
             else:
                 late_raw[row : row + 1, :] = values
-            quant[group, row : row + 1, :] = rounded(quantile_ref[b : b + 1, :])
 
     for d in range(date_slots):
         live = lax.rem(jnp.int32(d), date_slots) < live_ref[my_date]
@@ -376,6 +378,13 @@
     each_date_peer(lambda peer: raw_copy(peer, my_date).start())
     each_date_peer(lambda peer: mask_copy(peer, my_date).start())
 
+    for load in loads[3:]:
+        load.wait()
+    quant[...] = jnp.zeros_like(quant)
+    for d in range(date_slots):
+        for b in range(bands):
+            group, row = find_row(d, b, bands)
+            quant[group, row : row + 1, :] = rounded(quantile_ref[b : b + 1, :])
     fit_rows = own_fit_rows(live_ref, day_ref, date_slots, dates, my_date * date_slots)
 
     total = [hist_own[d] for d in range(date_slots)]

time: 13.6 us -> 13.6 us (level)
  no operation moved by 1% of the time
where the time goes in v9:
time: 13.6 us; the launch traced here: 13.5 us
  Pallas kernels  12.9 us (95%)
  local copies, waits for them, and re-layouts  0.62 us (5%)
    pallas_call x1, Pallas kernels, per_device(): pl.pallas_call(functools.partial(kernel, groups, spaces), out_shape=jax.S...  12.9 us
    unnamed x1, local copies, waits for them, and re-layouts  0.62 us

profile of v9, /device:TPU:0, one launch (start us, length us, event | category | flops | bytes accessed | tf_op | source)
XLA Modules:
  0.0 13.5 jit_solution(15133125956013323040)
XLA Ops:
  0.0 12.9 %shard_map.55 = f32[6,2,1024]{2,1,0:T(2,128)S(1)} custom-call(s32[4]{0:T(128)} %live_hbm.1, s32[8]{0:T(128)} %day_hbm.1, f32[6,2,1024]{2,1,0:T(2,128)} %bitcast.3, s32[2,1024]{1,0:T(2,128)} %clear_hbm.1, f32[6,256]{1,0:T(8,128)} %quantile_hbm.1), custom_call_target="tpu_custom_call" | custom-call | tf_op jit(solution)/shard_map/pallas_call | solution.py:494
  12.9 0.6 %copy.7 = f32[2,6,1024]{2,0,1:T(2,128)} copy(f32[2,6,1024]{2,0,1:T(2,128)S(1)} %bitcast.2) | data formatting | bytes 98304

commit v10 on v9

--- a/solution.py
+++ b/solution.py
@@ -262,14 +262,14 @@
 
     def each_date_peer(body):
         def step(i, carry):
-            body(lax.rem(my_date + i, groups))
+            body(i + jnp.where(my_date <= i, 1, 0))
             return carry
 
         if groups <= 8:
-            for i in range(1, groups):
+            for i in range(groups - 1):
                 step(i, 0)
         else:
-            lax.fori_loop(1, groups, step, 0)
+            lax.fori_loop(0, groups - 1, step, 0)
 
     def to_date(src, dst, send, recv, peer):
         return pltpu.make_async_remote_copy(
@@ -375,8 +375,12 @@
         )
         copy.start()
         hist_copies.append(copy)
-    each_date_peer(lambda peer: raw_copy(peer, my_date).start())
-    each_date_peer(lambda peer: mask_copy(peer, my_date).start())
+
+    def send_raw(peer):
+        raw_copy(peer, my_date).start()
+        mask_copy(peer, my_date).start()
+
+    each_date_peer(send_raw)
 
     for load in loads[3:]:
         load.wait()

time: 13.6 us -> 13.6 us (level)
  no operation moved by 1% of the time
where the time goes in v10:
time: 13.6 us; the launch traced here: 13.5 us
  Pallas kernels  12.9 us (95%)
  local copies, waits for them, and re-layouts  0.62 us (5%)
    pallas_call x1, Pallas kernels, per_device(): pl.pallas_call(functools.partial(kernel, groups, spaces), out_shape=jax.S...  12.9 us
    unnamed x1, local copies, waits for them, and re-layouts  0.62 us

profile of v10, /device:TPU:0, one launch (start us, length us, event | category | flops | bytes accessed | tf_op | source)
XLA Modules:
  0.0 13.5 jit_solution(14767736544899908393)
XLA Ops:
  0.0 12.9 %shard_map.55 = f32[6,2,1024]{2,1,0:T(2,128)S(1)} custom-call(s32[4]{0:T(128)} %live_hbm.1, s32[8]{0:T(128)} %day_hbm.1, f32[6,2,1024]{2,1,0:T(2,128)} %bitcast.3, s32[2,1024]{1,0:T(2,128)} %clear_hbm.1, f32[6,256]{1,0:T(8,128)} %quantile_hbm.1), custom_call_target="tpu_custom_call" | custom-call | tf_op jit(solution)/shard_map/pallas_call | solution.py:498
  12.9 0.6 %copy.7 = f32[2,6,1024]{2,0,1:T(2,128)} copy(f32[2,6,1024]{2,0,1:T(2,128)S(1)} %bitcast.2) | data formatting | bytes 98304

commit v11 on v10

--- a/solution.py
+++ b/solution.py
@@ -342,6 +342,15 @@
         valid = clear_ref[d : d + 1, :] * live.astype(jnp.int32)
         mask_all[my_date, d : d + 1, :] = valid.astype(jnp.float32)
 
+    def send_raw(peer):
+        raw_copy(peer, my_date).start()
+        mask_copy(peer, my_date).start()
+
+    @pl.when(my_date >= groups // 2)
+    def _():
+        pl.semaphore_wait(barrier, groups + spaces - 2)
+        each_date_peer(send_raw)
+
     def row_mask(slot, span):
         size = span.stop - span.start
         slots, _ = row_slot_band(iota((SUBLANES, size), 0), bands)
@@ -361,7 +370,9 @@
     for d in range(date_slots):
         hist_own[d] = sums[d]
 
-    pl.semaphore_wait(barrier, groups + spaces - 2)
+    @pl.when(my_date < groups // 2)
+    def _():
+        pl.semaphore_wait(barrier, groups + spaces - 2)
 
     hist_copies = []
     for peer in space_peers:
@@ -376,11 +387,9 @@
         copy.start()
         hist_copies.append(copy)
 
-    def send_raw(peer):
-        raw_copy(peer, my_date).start()
-        mask_copy(peer, my_date).start()
-
-    each_date_peer(send_raw)
+    @pl.when(my_date < groups // 2)
+    def _():
+        each_date_peer(send_raw)
 
     for load in loads[3:]:
         load.wait()

time: 13.6 us -> 14 us (1.029)
  Pallas kernels: 12.9 us -> 13.3 us
    pallas_call x1, Pallas kernels: 12.9 us -> 13.3 us  [per_device(): pl.pallas_call(functools.partial(kernel, groups, spaces), out_shape=jax.S...]
where the time goes in v11:
time: 14 us; the launch traced here: 13.9 us
  Pallas kernels  13.3 us (95%)
  local copies, waits for them, and re-layouts  0.62 us (4%)
    pallas_call x1, Pallas kernels, per_device(): pl.pallas_call(functools.partial(kernel, groups, spaces), out_shape=jax.S...  13.3 us
    unnamed x1, local copies, waits for them, and re-layouts  0.62 us

profile of v11, /device:TPU:0, one launch (start us, length us, event | category | flops | bytes accessed | tf_op | source)
XLA Modules:
  0.0 13.9 jit_solution(11591545325423941574)
XLA Ops:
  0.0 13.3 %shard_map.55 = f32[6,2,1024]{2,1,0:T(2,128)S(1)} custom-call(s32[4]{0:T(128)} %live_hbm.1, s32[8]{0:T(128)} %day_hbm.1, f32[6,2,1024]{2,1,0:T(2,128)} %bitcast.3, s32[2,1024]{1,0:T(2,128)} %clear_hbm.1, f32[6,256]{1,0:T(8,128)} %quantile_hbm.1), custom_call_target="tpu_custom_call" | custom-call | tf_op jit(solution)/shard_map/pallas_call | solution.py:507
  13.3 0.6 %copy.7 = f32[2,6,1024]{2,0,1:T(2,128)} copy(f32[2,6,1024]{2,0,1:T(2,128)S(1)} %bitcast.2) | data formatting | bytes 98304
